TPU v7x, 128 devices: a whole 4x4x4 slice. The times are simulated.
128 devices in a mesh: patch: 64 (over z, y, x), batch: 2 (over core).
Axes of the slice: x: 4, y: 4, z: 4, core: 2. Of those that a mesh axis runs over, the one named last changes fastest.
Arguments:
- tokens: bfloat16 [16384, 1152], P(('batch', 'patch')), parts along dimension 0, may hold values from -6 to 6
- slots: int32 [16384], P(('batch', 'patch')), parts along dimension 0, may hold values from 0 to 127, as said below
- counts: int32 [128], P(('batch', 'patch')), parts along dimension 0, may hold values from 32 to 128, as said below
- shift: float32 [1152], replicated, may hold values from -3 to 3
- scale: float32 [1152], replicated, may hold values from -3 to 3
- gate: float32 [1152], replicated, may hold values from -4 to 4
- w_qkv: bfloat16 [1152, 3456], replicated, may hold values from -1 to 1
- w_out: bfloat16 [1152, 1152], replicated, may hold values from -0.1875 to 0.1875
Outputs:
- result: bfloat16 [16384, 1152], P(('batch', 'patch')), parts along dimension 0
There are 2 independent parts, one for each index of `batch`. A program takes and returns all parts, laid end to end along the dimension named above; an argument that names none is the same for every part. Nothing has to cross between parts.
Inputs may be any that keep to these rules, and one draw needn't show every extreme that they name: `counts`: at least a quarter of each block's slots are live. The live slots of all blocks of an image number exactly 80 times the number of patch devices, and all blocks of some device are full. `slots`: every token's slot is below its block's count, and every slot below the count holds at least one token.
All inputs are finite; a program needn't handle non-finite values.
Results may differ from a plain program's by a relative error of at most 0.011.
Values may be sent and summed in bfloat16 or wider, within the bound.
No kernel may reach another device: no remote copies, remote signals or barrier semaphores. Data moves between devices by JAX's collectives and lax.ppermute only.
A program may use at most 192 MiB of HBM per device.

v0:
```python
import math

import jax
import jax.numpy as jnp
from jax import lax
from jax.sharding import PartitionSpec as P

HEADS = 16
BLK = 128


def laid_out(parts, dim):
    parts = jnp.moveaxis(parts, 0, dim)
    dims = parts.shape
    return parts.reshape(*dims[:dim], dims[dim] * dims[dim + 1], *dims[dim + 2 :])


def from_everyone(value, axis):
    length = lax.axis_size(axis)
    return lax.all_to_all(
        jnp.broadcast_to(value[None], (length, *value.shape)), axis, 0, 0, tiled=True
    )


def gather_directly(value, axis, dim):
    return laid_out(from_everyone(value, axis), dim)


def side_by_side(arrays, axis, split_dim, concat_dim, along):
    widths = [math.prod(a.shape[along:]) for a in arrays]
    both = jnp.concatenate(
        [a.reshape(*a.shape[:along], w) for a, w in zip(arrays, widths)], axis=along
    )
    out = lax.all_to_all(both, axis, split_axis=split_dim, concat_axis=concat_dim, tiled=True)
    parts = jnp.split(out, [sum(widths[:k]) for k in range(1, len(widths))], axis=along)
    return tuple((b.reshape(*out.shape[:along], *a.shape[along:]) for a, b in zip(arrays, parts)))


def in_one_piece(arrays, axis, dim, along):
    columns = [a.reshape(*a.shape[:along], -1) for a in arrays]
    both = jnp.concatenate(columns, axis=along)
    out, at, done = (lax.all_gather(both, axis, axis=dim, tiled=True), 0, [])
    for a, column in zip(arrays, columns):
        share = out[..., at : at + column.shape[along]]
        done.append(share.reshape(*share.shape[:along], *a.shape[along:]))
        at += column.shape[along]
    return tuple(done)


def layer_norm(merged, shift, scale):
    values = merged.astype(jnp.float32)
    center = jnp.mean(values, axis=-1, keepdims=True)
    spread = jnp.mean((values - center) ** 2, axis=-1, keepdims=True)
    return ((values - center) * lax.rsqrt(spread + 1e-06) * (1.0 + scale) + shift).astype(
        jnp.bfloat16
    )


def size_bias(sizes):
    return jnp.log(jnp.maximum(sizes.astype(jnp.float32), 1.0))


def empty_carry(heads, query_rows, head_size):
    return (
        jnp.full((heads, query_rows), -1e30, jnp.float32),
        jnp.zeros((heads, query_rows), jnp.float32),
        jnp.zeros((heads, query_rows, head_size), jnp.float32),
    )


def finish(accum, total):
    heads, query_rows, head_size = accum.shape
    return (
        (accum / total[:, :, None])
        .transpose(1, 0, 2)
        .reshape(query_rows, heads * head_size)
        .astype(jnp.bfloat16)
    )


def attend_piece(query, carry, keys, values, bias, inverse):
    top, total, accum = carry
    key_rows = keys.shape[0]
    heads = query.shape[1]
    key_heads = keys.reshape(key_rows, heads, -1)
    value_heads = values.reshape(key_rows, heads, -1)
    score = (
        jnp.einsum("qhe,khe->hqk", query, key_heads, preferred_element_type=jnp.float32) * inverse
        + bias[None, None, :]
    )
    new_top = jnp.maximum(top, jnp.max(score, axis=-1))
    probs = jnp.exp(score - new_top[:, :, None])
    total = jnp.sum(probs, axis=-1)
    update = jnp.einsum(
        "hqk,khe->hqe", probs.astype(jnp.bfloat16), value_heads, preferred_element_type=jnp.float32
    )
    return (new_top, total, update)


def body(tokens, slots, counts, shift, scale, gate, w_qkv, w_out):
    rows, width = tokens.shape
    nblk = rows // BLK
    heads = HEADS
    head_size = width // heads
    inverse = 1.0 / head_size**0.5
    nothing = jnp.zeros((), jnp.bfloat16)
    onehot = slots.reshape(nblk, BLK)[:, :, None] == jnp.arange(BLK, dtype=jnp.int32)[None, None, :]
    sums = jnp.einsum(
        "bts,btd->bsd",
        onehot.astype(jnp.bfloat16),
        tokens.reshape(nblk, BLK, width),
        preferred_element_type=jnp.float32,
    )
    members = jnp.sum(onehot.astype(jnp.float32), axis=1)
    merged = (
        (sums / jnp.maximum(members, 1.0)[:, :, None]).astype(jnp.bfloat16).reshape(rows, width)
    )
    normed = layer_norm(merged, shift, scale)
    sizes = members.reshape(rows).astype(jnp.bfloat16)
    count = lax.axis_size("patch")
    me = lax.axis_index("patch")
    every_count = gather_directly(counts, "patch", 0)
    loads = jnp.sum(every_count.reshape(count, nblk), axis=1)
    ends = jnp.cumsum(loads)
    starts = ends - loads
    devices = jnp.arange(count, dtype=jnp.int32)
    own_start = jnp.sum(jnp.where(devices == me, starts, 0))
    own_load = jnp.sum(counts)
    share = 5 * rows // 8
    capacity = (rows + count - 2) // count + 1
    block_ends = jnp.cumsum(counts)
    block_starts = block_ends - counts
    blocks = jnp.arange(nblk, dtype=jnp.int32)
    place = jnp.arange(capacity, dtype=jnp.int32)
    position = (
        (own_start // count + place[None, :]) * count + devices[:, None] - own_start
    ).reshape(count * capacity)
    sent_valid = (position >= 0) & (position < own_load)
    block_of = jnp.sum((position[:, None] >= block_ends[None, :]).astype(jnp.int32), axis=1)
    start_of = jnp.sum(
        jnp.where(block_of[:, None] == blocks[None, :], block_starts[None, :], 0), axis=1
    )
    source_row = jnp.clip(block_of * BLK + position - start_of, 0, rows - 1)
    sent_rows = jnp.where(sent_valid[:, None], jnp.take(normed, source_row, axis=0), nothing)
    sent_sizes = jnp.where(sent_valid, jnp.take(sizes, source_row, axis=0), nothing)
    got_rows, got_sizes = side_by_side(
        (sent_rows.reshape(count, capacity, width), sent_sizes.reshape(count, capacity)),
        "patch",
        0,
        0,
        2,
    )
    ranking = jnp.arange(share, dtype=jnp.int32)
    global_place = ranking * count + me
    source = jnp.sum((global_place[:, None] >= ends[None, :]).astype(jnp.int32), axis=1)
    source_start = jnp.sum(
        jnp.where(source[:, None] == devices[None, :], starts[None, :], 0), axis=1
    )
    slot_index = source * capacity + ranking - source_start // count
    live_rows = jnp.take(got_rows.reshape(count * capacity, width), slot_index, axis=0)
    live_sizes = jnp.take(got_sizes.reshape(count * capacity), slot_index, axis=0)
    qkv = jnp.dot(live_rows, w_qkv, preferred_element_type=jnp.float32)
    query = qkv[:, :width].astype(jnp.bfloat16)
    keys = qkv[:, width : 2 * width].astype(jnp.bfloat16)
    values = qkv[:, 2 * width :].astype(jnp.bfloat16)
    query_heads = query.reshape(share, heads, head_size)
    keys_part, values_part, sizes_part = in_one_piece((keys, values, live_sizes), "patch", 0, 1)
    top, total, accum = attend_piece(
        query_heads,
        empty_carry(heads, share, head_size),
        keys_part,
        values_part,
        size_bias(sizes_part),
        inverse,
    )
    live_attended = finish(accum, total)
    back_rank = (starts // count)[:, None] + place[None, :]
    back_place = back_rank * count + me
    back_valid = ((back_place >= starts[:, None]) & (back_place < ends[:, None])).reshape(
        count * capacity
    )
    back_rows = jnp.where(
        back_valid[:, None],
        jnp.take(
            live_attended, jnp.clip(back_rank.reshape(count * capacity), 0, share - 1), axis=0
        ),
        nothing,
    )
    returned = lax.all_to_all(
        back_rows.reshape(count, capacity, width), "patch", split_axis=0, concat_axis=0, tiled=True
    )
    slot_in_block = jnp.arange(rows, dtype=jnp.int32) % BLK
    row_counts = jnp.broadcast_to(counts[:, None], (nblk, BLK)).reshape(rows)
    row_starts = jnp.broadcast_to(block_starts[:, None], (nblk, BLK)).reshape(rows)
    row_alive = slot_in_block < row_counts
    row_place = own_start + row_starts + slot_in_block
    home_index = jnp.clip(
        row_place % count * capacity + row_place // count - own_start // count,
        0,
        count * capacity - 1,
    )
    attended = jnp.where(
        row_alive[:, None],
        jnp.take(returned.reshape(count * capacity, width), home_index, axis=0),
        nothing,
    )
    projected = jnp.dot(attended, w_out, preferred_element_type=jnp.float32)
    branch = jnp.einsum(
        "bts,bsd->btd", onehot.astype(jnp.float32), projected.reshape(nblk, BLK, width)
    ).reshape(rows, width)
    return (tokens.astype(jnp.float32) + gate * branch).astype(jnp.bfloat16)


def solution(mesh):
    return jax.shard_map(
        body,
        mesh=mesh,
        in_specs=(
            P(("batch", "patch"), None),
            P(("batch", "patch")),
            P(("batch", "patch")),
            P(),
            P(),
            P(),
            P(),
            P(),
        ),
        out_specs=P(("batch", "patch"), None),
        check_vma=False,
    )
```

profile of v0, /device:TPU:0, one launch (start us, length us, event | category | flops | bytes accessed | tf_op | source)
XLA Modules:
  0.0 330.5 jit_solution(15551254633294351243)
XLA Ops:
  8.0 11.5 %all-to-all-start = ((s32[64,1,1]{2,1,0:T(1,128)}), s32[64,1,1]{2,1,0:T(1,128)S(1)}, u32[]{:S(2)}, u32[]{:S(2)}) async-start(s32[64,1,1]{2,1,0:T(1,128)} %broadcast_in_dim.155), calls=%async_computation | async-start | bytes 65536 | tf_op jit(solution)/shard_map/all_to_all | solution.py:20
  20.9 1.4 fusion.73
  23.5 5.4 %all-to-all-done = s32[64,1,1]{2,1,0:T(1,128)S(1)} async-done(((s32[64,1,1]{2,1,0:T(1,128)}), s32[64,1,1]{2,1,0:T(1,128)S(1)}, u32[]{:S(2)}, u32[]{:S(2)}) %all-to-all-start) | async-done | bytes 288 | tf_op jit(solution)/shard_map/all_to_all | solution.py:20
  29.2 1.2 reduce.2
  36.0 1.6 gather_fusion.1
  37.8 1.8 gather_fusion
  39.7 1.5 gather.33
  41.2 0.9 fusion.41
  42.6 1.1 pad_maximum_fusion
  43.7 5.0 %all-to-all-start.1 = ((bf16[64,3,1153]{2,1,0:T(4,128)(2,1)}), bf16[64,3,1153]{2,1,0:T(4,128)(2,1)S(1)}, u32[]{:S(2)}, u32[]{:S(2)}) async-start(bf16[64,3,1153]{2,1,0:T(4,128)(2,1)} %pad_maximum_fusion), calls=%async_computation.1 | async-start | bytes 1310720 | tf_op jit(solution)/shard_map/all_to_all | solution.py:34
  48.9 13.9 %all-to-all-done.1 = bf16[64,3,1153]{2,1,0:T(4,128)(2,1)S(1)} async-done(((bf16[64,3,1153]{2,1,0:T(4,128)(2,1)}), bf16[64,3,1153]{2,1,0:T(4,128)(2,1)S(1)}, u32[]{:S(2)}, u32[]{:S(2)}) %all-to-all-start.1) | async-done | bytes 442784 | tf_op jit(solution)/shard_map/all_to_all | solution.py:34
  63.7 1.0 split.8
  64.7 1.4 reshape.768
  66.1 1.0 slice_reduce_fusion
  68.1 1.2 gather_fusion.3
  69.4 4.6 %convolution_convert_fusion = bf16[80,3456]{1,0:T(8,128)(2,1)S(1)} fusion(bf16[1152,3456]{1,0:T(8,128)(2,1)} %param.14, bf16[80,1152]{1,0:T(8,128)(2,1)S(1)} %gather_fusion.2, pred[80]{0:T(512)(128)(4,1)S(1)} %compare_and_fusion.1), kind=kOutput, calls=%fused_computation.15 | convolution fusion | flops 637378560 | bytes 8699984 | tf_op jit(solution)/shard_map/dot_general | solution.py:162
  75.7 126.0 %all-gather.2.cloned.1.call-done = bf16[5120,2305]{1,0:T(8,128)(2,1)} async-done(((bf16[80,2305]{1,0:T(8,128)(2,1)}), bf16[5120,2305]{1,0:T(8,128)(2,1)}) %all-gather.2.cloned.1.call-update) | async-done | bytes 23603216 | tf_op jit(solution)/shard_map/all_gather | solution.py:42
  201.7 16.7 %fusion.72 = (bf16[5120,1152]{1,0:T(8,128)(2,1)}, bf16[5120,1152]{1,0:T(8,128)(2,1)}) fusion(bf16[5120,2305]{1,0:T(8,128)(2,1)} %all-gather.2.cloned.1.call-done), kind=kLoop, calls=%fused_computation.140 | loop fusion | bytes 47185920 | tf_op jit(solution)/shard_map/slice | solution.py:44
  218.3 16.3 %copy.81 = bf16[5120,1152]{0,1:T(8,128)(2,1)} copy(bf16[5120,1152]{1,0:T(8,128)(2,1)} %get-tuple-element.9) | data formatting | bytes 23592960 | tf_op jit(solution)/shard_map/slice | solution.py:44
  234.7 16.3 %copy.83 = bf16[5120,1152]{0,1:T(8,128)(2,1)} copy(bf16[5120,1152]{1,0:T(8,128)(2,1)} %get-tuple-element.10) | data formatting | bytes 23592960 | tf_op jit(solution)/shard_map/slice | solution.py:44
  251.0 2.1 log_reduce_fusion
  253.0 13.4 %fusion = (f32[16,80]{1,0:T(8,128)S(1)}, f32[16,80,5120]{2,1,0:T(8,128)}) fusion(f32[5120]{0:T(1024)S(1)} %log_reduce_fusion, bf16[80,16,72]{0,2,1:T(8,128)(2,1)S(1)} %bitcast.34, bf16[5120,16,72]{0,2,1:T(8,128)(2,1)} %bitcast.32), kind=kOutput, calls=%fused_computation.8 | convolution fusion | flops 963377920 | bytes 38220800 | tf_op jit(solution)/shard_map/qhe,khe->hqk/dot_general | solution.py:88
  266.5 9.7 %fusion.1 = f32[16,80]{1,0:T(8,128)S(1)} fusion(f32[16,80,5120]{2,1,0:T(8,128)} %get-tuple-element.20, f32[16,80]{1,0:T(8,128)S(1)} %broadcast_maximum_fusion, f32[5120]{0:T(1024)S(1)} %log_reduce_fusion), kind=kLoop, calls=%fused_computation.9 | loop fusion | flops 26213120 | bytes 26245120 | tf_op jit(solution)/shard_map/reduce_sum | solution.py:93
  276.2 14.7 %fusion.20 = bf16[80,16,72]{0,2,1:T(8,128)(2,1)S(1)} fusion(bf16[5120,16,72]{0,2,1:T(8,128)(2,1)} %bitcast.33, f32[16,80,5120]{2,1,0:T(8,128)} %get-tuple-element.20, f32[16,80]{1,0:T(8,128)S(1)} %broadcast_maximum_fusion, f32[5120]{0:T(1024)S(1)} %log_reduce_fusion, f32[80,16]{0,1:T(8,128)S(1)} %bitcast.37), kind=kOutput, calls=%fused_computation.26 | convolution fusion | flops 970117120 | bytes 38225920 | tf_op jit(solution)/shard_map/hqk,khe->hqe/dot_general | solution.py:94
  291.1 1.8 gather_fusion.4
  292.9 1.7 gather.40
  294.6 1.3 select_select_fusion
  296.0 8.9 %all-to-all-start.2 = ((bf16[64,3,1152]{2,1,0:T(4,128)(2,1)}), bf16[64,3,1152]{2,1,0:T(4,128)(2,1)}, u32[]{:S(2)}, u32[]{:S(2)}) async-start(bf16[64,3,1152]{2,1,0:T(4,128)(2,1)} %select_select_fusion), calls=%async_computation.2 | async-start | bytes 1179648 | tf_op jit(solution)/shard_map/all_to_all | solution.py:189
  306.2 12.6 %all-to-all-done.2 = bf16[64,3,1152]{2,1,0:T(4,128)(2,1)} async-done(((bf16[64,3,1152]{2,1,0:T(4,128)(2,1)}), bf16[64,3,1152]{2,1,0:T(4,128)(2,1)}, u32[]{:S(2)}, u32[]{:S(2)}) %all-to-all-start.2) | async-done | bytes 442400 | tf_op jit(solution)/shard_map/all_to_all | solution.py:189
  318.8 1.4 reshape.772
  320.2 0.9 gather_fusion.5
  321.1 2.5 fusion.11
  (64 shorter events, 12.3 us)
Async XLA Ops:
  6.5 314.6 %copy-start = (bf16[1152,1152]{1,0:T(8,128)(2,1)S(1)}, bf16[1152,1152]{1,0:T(8,128)(2,1)}, u32[]{:S(2)}) copy-start(bf16[1152,1152]{1,0:T(8,128)(2,1)} %param.15) | copy-start | bytes 7962628
  8.0 21.0 %all-to-all-start = ((s32[64,1,1]{2,1,0:T(1,128)}), s32[64,1,1]{2,1,0:T(1,128)S(1)}, u32[]{:S(2)}, u32[]{:S(2)}) async-start(s32[64,1,1]{2,1,0:T(1,128)} %broadcast_in_dim.155), calls=%async_computation | async-start | bytes 65536 | tf_op jit(solution)/shard_map/all_to_all | solution.py:20
  43.7 19.1 %all-to-all-start.1 = ((bf16[64,3,1153]{2,1,0:T(4,128)(2,1)}), bf16[64,3,1153]{2,1,0:T(4,128)(2,1)S(1)}, u32[]{:S(2)}, u32[]{:S(2)}) async-start(bf16[64,3,1153]{2,1,0:T(4,128)(2,1)} %pad_maximum_fusion), calls=%async_computation.1 | async-start | bytes 1310720 | tf_op jit(solution)/shard_map/all_to_all | solution.py:34
  48.7 153.0 %all-gather.2.cloned.1.call-start = ((), (), s32[]{:S(2)}) async-start(), calls=%async_computation.3 | async-start | bytes 25292800 | tf_op jit(solution)/shard_map/all_gather | solution.py:42
  62.8 0.8 copy-start.1
  276.2 45.0 %copy-start.2 = (f32[1152]{0:T(1024)S(1)}, f32[1152]{0:T(1024)}, u32[]{:S(2)}) copy-start(f32[1152]{0:T(1024)} %param.13) | copy-start | bytes 13828
  276.2 45.0 %copy-start.3 = (s32[128]{0:T(128)S(1)}, s32[128]{0:T(128)}, u32[]{:S(2)}) copy-start(s32[128]{0:T(128)} %param.9) | copy-start | bytes 1540
  296.0 22.8 %all-to-all-start.2 = ((bf16[64,3,1152]{2,1,0:T(4,128)(2,1)}), bf16[64,3,1152]{2,1,0:T(4,128)(2,1)}, u32[]{:S(2)}, u32[]{:S(2)}) async-start(bf16[64,3,1152]{2,1,0:T(4,128)(2,1)} %select_select_fusion), calls=%async_computation.2 | async-start | bytes 1179648 | tf_op jit(solution)/shard_map/all_to_all | solution.py:189
Sparse Core Ops, SparseCore 0:
  75.1 126.5 all-gather.1
where the time goes:
time: 332 us; the launch traced here: 330 us
  waiting for transfers between devices  158 us (48%)
  local copies, waits for them, and re-layouts  69.1 us (21%)
  matrix products  36.7 us (11%)
  starting transfers between devices  25.4 us (8%)
  other arithmetic  24.3 us (7%)
  between operations  17.1 us (5%)
    all_gather x1, waiting for transfers between devices, in_one_piece(): out, at, done = (lax.all_gather(both, axis, axis=dim, tiled=True), 0, [])  126 us
    slice x3, local copies, waits for them, and re-layouts, in_one_piece(): share = out[..., at:at + column.shape[along]]  49.3 us
    dot_general x1, matrix products, attend_piece(): jnp.einsum('hqk,khe->hqe', probs.astype(jnp.bfloat16), value_heads, prefe...  14.7 us
    all_to_all x1, waiting for transfers between devices, side_by_side(): lax.all_to_all(both, axis, split_axis=split_dim, concat_axis=concat_dim,...  13.9 us
    dot_general x1, matrix products, attend_piece(): jnp.einsum('qhe,khe->hqk', query, key_heads, preferred_element_type=jnp.f...  13.4 us
    all_to_all x1, waiting for transfers between devices, body(): lax.all_to_all(back_rows.reshape(count, capacity, width), 'patch', split_...  12.6 us
    all_to_all x1, starting transfers between devices, from_everyone(): lax.all_to_all(jnp.broadcast_to(value[None], (length, *value.shape)), axi...  11.5 us
    reduce_sum x1, other arithmetic, attend_piece(): total = jnp.sum(probs, axis=-1)  9.67 us
  transfers between devices with their start and end apart: 4, of which 4 were waited for; matrix products, arithmetic and copies ran while one was open for 2% of the time, Pallas kernels for 0%

commit v1 on v0

v1 whole, which is shorter than its diff:
```python
import jax
import jax.numpy as jnp
from jax import lax
from jax.experimental import pallas as pl
from jax.experimental.pallas import tpu as pltpu
from jax.sharding import PartitionSpec as P

D = 1152
HEADS = 16
HD = 72
BLK = 128
HALF = BLK // 2
DEVICES = 64
GROUPS = DEVICES // HEADS

IN_ROWS = 112
OUT_ROWS = 40
AUG = 80
TILES = 22
WIDE = 2 * BLK
COLUMNS = TILES * BLK
W_CHUNK = 384
W_CHUNKS = 3 * D // W_CHUNK
VMEM = 56 * 1024 * 1024

INVERSE = 1.0 / HD**0.5
LOG2E = 1.4426950408889634


def place_of(slots):
    return (slots & 1) * HALF + (slots >> 1)


def roll(x, shift):
    return pltpu.roll(x, shift, 1)


def pre_kernel(
    counts_ref, slots_ref, tokens_ref, shift_ref, scale_ref, w_ref, out_ref, w_buf, qkv_t, sems
):
    copies = [
        pltpu.make_async_copy(
            w_ref.at[:, pl.ds(c * W_CHUNK, W_CHUNK)], w_buf.at[c], sems.at[c]
        )
        for c in range(W_CHUNKS)
    ]
    for copy in copies:
        copy.start()
    place = jnp.broadcast_to(place_of(slots_ref[...]), (BLK, BLK))
    row_id = lax.broadcasted_iota(jnp.int32, (BLK, BLK), 0)
    hot = jnp.where(place == row_id, 1.0, 0.0)
    members = jnp.sum(hot, axis=1, keepdims=True)
    sums = jnp.dot(hot.astype(jnp.bfloat16), tokens_ref[...], preferred_element_type=jnp.float32)
    values = (sums / jnp.maximum(members, 1.0)).astype(jnp.bfloat16).astype(jnp.float32)
    center = jnp.mean(values, axis=-1, keepdims=True)
    off = values - center
    spread = jnp.mean(off * off, axis=-1, keepdims=True)
    normed = (off * lax.rsqrt(spread + 1e-06) * (1.0 + scale_ref[...]) + shift_ref[...]).astype(
        jnp.bfloat16
    )
    for c in range(W_CHUNKS):
        copies[c].wait()
        part = jnp.dot(normed, w_buf[c], preferred_element_type=jnp.float32)
        for t in range(W_CHUNK // BLK):
            at = c * W_CHUNK + t * BLK
            qkv_t[at : at + BLK, :] = part[:, t * BLK : (t + 1) * BLK].T

    members_row = jnp.sum(hot.T, axis=0, keepdims=True)
    low = lax.broadcasted_iota(jnp.int32, (1, BLK), 1) < HALF
    line = lax.broadcasted_iota(jnp.int32, (8, BLK), 0)
    count = counts_ref[0]
    live = [((count + 1) >> 1).astype(jnp.float32), (count >> 1).astype(jnp.float32)]
    sizes_of = [roll(jnp.broadcast_to(members_row, (8, BLK)), HALF)]
    sizes_of.append(jnp.broadcast_to(members_row, (8, BLK)))
    sizes = [
        [
            jnp.where(
                line == 0,
                sizes_of[b],
                jnp.where(line == 1, live[b], jnp.where(line == 2, live[a], 0.0)),
            )
            for b in range(2)
        ]
        for a in range(2)
    ]
    for h in range(HEADS):
        q = qkv_t[h * HD : (h + 1) * HD, :]
        k = qkv_t[D + h * HD : D + (h + 1) * HD, :]
        v = qkv_t[2 * D + h * HD : 2 * D + (h + 1) * HD, :]
        q_roll, k_roll, v_roll = roll(q, HALF), roll(k, HALF), roll(v, HALF)
        kv = [jnp.where(low, k, v_roll), jnp.where(low, k_roll, v)]
        q_pair = [
            jnp.where(low, q[:32], q_roll[32:64]),
            jnp.where(low, q_roll[:32], q[32:64]),
        ]
        q_last = [q[64:], q_roll[64:]]
        for a in range(2):
            for b in range(2):
                last = jnp.where(low, q_last[a], sizes[a][b])
                out_ref[h * GROUPS + 2 * a + b] = jnp.concatenate(
                    [kv[b], q_pair[a], last], axis=0
                ).astype(jnp.bfloat16)


def attend_kernel(
    got_ref,
    out_ref,
    offs_v,
    offs,
    k_t,
    v_t,
    q_t,
    keys,
    vals,
    queries,
    scores,
    probs,
    done_t,
    sem,
):
    lane = lax.broadcasted_iota(jnp.int32, (1, BLK), 1)
    low = lane < HALF

    row = lax.broadcasted_iota(jnp.int32, (144, DEVICES * 16), 0)
    col = lax.broadcasted_iota(jnp.int32, (144, DEVICES * 16), 1)
    is_q = row >= 72
    index = jnp.where(is_q, row - 72, row)
    line = jnp.where(is_q, 10, 9)
    before = ((col & 15) == line) & ((col >> 4) < index)
    tail = got_ref[:, IN_ROWS - 16 :, :].reshape(DEVICES * 16, BLK)
    offs_v[...] = jnp.dot(
        jnp.where(before, 1.0, 0.0).astype(jnp.bfloat16), tail, preferred_element_type=jnp.float32
    ).astype(jnp.int32)
    copy = pltpu.make_async_copy(offs_v, offs, sem)
    copy.start()
    copy.wait()

    def put(dst, tile, first, last, moved, keep):
        dst[tile, first:last, :] = jnp.where(keep, moved, dst[tile, first:last, :])
        dst[tile + 1, first:last, :] = moved

    k_t[0] = jnp.zeros_like(k_t[0])
    v_t[0] = jnp.zeros_like(v_t[0])
    q_t[0] = jnp.zeros_like(q_t[0])

    def pack(b, _):
        k_at = offs[b, HALF]
        q_at = offs[72 + b, HALF]
        k_tile, k_off = k_at >> 7, k_at & 127
        q_tile, q_off = q_at >> 7, q_at & 127
        message = got_ref[b].astype(jnp.float32)
        keep_k, keep_q = lane >= k_off, lane >= q_off
        k_over, q_over = (k_off + HALF) & 127, (q_off + HALF) & 127
        put(k_t, k_tile, 0, HD, roll(message[:HD], k_off), keep_k)
        put(v_t, k_tile, 0, HD, roll(message[:HD], k_over), keep_k)
        put(k_t, k_tile, HD, AUG, roll(message[104:], k_over), keep_k)
        put(q_t, q_tile, 0, 32, roll(message[HD:104], q_off), keep_q)
        put(q_t, q_tile, 32, 64, roll(message[HD:104], q_over), keep_q)
        put(q_t, q_tile, 64, HD, roll(message[104:], q_off), keep_q)
        return 0

    lax.fori_loop(0, DEVICES, pack, 0, unroll=2)

    total = offs[64, HALF]
    line8 = lax.broadcasted_iota(jnp.int32, (8, BLK), 0)
    zeros = jnp.zeros((BLK - AUG, BLK), jnp.float32)
    ones2 = jnp.where(line8 < 2, 1.0, 0.0)
    ones1 = jnp.where(line8 < 1, 1.0, 0.0)
    written = TILES - 1
    for t in range(TILES):
        if t < written:
            members = jnp.broadcast_to(k_t[t, HD : HD + 1, :], (8, BLK))
            bias = jnp.log(jnp.maximum(members, 1.0)) * (1.0 / INVERSE)
            bias = jnp.where(lane + t * BLK < total, bias, -1e30)
            high = bias.astype(jnp.bfloat16).astype(jnp.float32)
            rest = jnp.where(line8 == 0, high, jnp.where(line8 == 1, bias - high, 0.0))
            k_tile, v_tile, q_tile = k_t[t, :HD, :], v_t[t, :HD, :], q_t[t, :HD, :]
        else:
            rest = jnp.where(line8 == 0, -1e30, 0.0)
            k_tile = v_tile = q_tile = jnp.zeros((HD, BLK), jnp.float32)
        cols = slice(t * BLK, (t + 1) * BLK)
        keys[cols, :] = jnp.concatenate([k_tile, rest, zeros], axis=0).T.astype(jnp.bfloat16)
        vals[:, cols] = jnp.concatenate([v_tile, ones1], axis=0).astype(jnp.bfloat16)
        queries[t // 2, :, (t % 2) * BLK : (t % 2 + 1) * BLK] = jnp.concatenate(
            [q_tile, ones2, zeros], axis=0
        ).astype(jnp.bfloat16)

    def attend(i, _):
        s = jnp.dot(keys[...], queries[i], preferred_element_type=jnp.float32)
        scores[...] = s
        top = jnp.max(s, axis=0, keepdims=True)
        probs[...] = jnp.exp2((scores[...] - top) * (INVERSE * LOG2E)).astype(jnp.bfloat16)
        o = jnp.dot(vals[...], probs[...], preferred_element_type=jnp.float32)
        mass = o[HD : HD + 1]
        lse = jnp.broadcast_to(top * INVERSE + jnp.log(mass), (8, WIDE))
        high = lse.astype(jnp.bfloat16).astype(jnp.float32)
        line = lax.broadcasted_iota(jnp.int32, (8, WIDE), 0)
        stats = jnp.where(line == 0, high, jnp.where(line == 1, lse - high, 0.0))
        o = jnp.concatenate([o[:HD] * (1.0 / mass), stats], axis=0)
        done_t[2 * i] = o[:, :BLK]
        done_t[2 * i + 1] = o[:, BLK:]
        return 0

    lax.fori_loop(0, TILES // 2, attend, 0)

    def unpack(b, _):
        at = offs[72 + b, HALF]
        tile, off = at >> 7, at & 127
        both = jnp.where(lane >= off, done_t[tile], done_t[tile + 1])
        first = roll(both[:OUT_ROWS], (BLK - off) & 127)
        second = roll(both[OUT_ROWS:], (BLK + HALF - off) & 127)
        out_ref[b] = jnp.where(low, first, second).astype(jnp.bfloat16)
        return 0

    lax.fori_loop(0, DEVICES, unpack, 0, unroll=2)


def post_kernel(got_ref, slots_ref, tokens_ref, gate_ref, w_ref, out_ref, att_t):
    low = lax.broadcasted_iota(jnp.int32, (1, BLK), 1) < HALF
    for h in range(HEADS):
        halves = []
        for a in range(2):
            parts = [got_ref[h * GROUPS + 2 * a + b].astype(jnp.float32) for b in range(2)]
            lse = [p[32:33] + p[33:34] for p in parts]
            gap = jnp.broadcast_to(lse[1] - lse[0], (8, BLK))
            gap = jnp.where(low, roll(gap, HALF), gap)[:1]
            share = 1.0 / (1.0 + jnp.exp(gap))
            halves.append(parts[0] * share + parts[1] * (1.0 - share))
        x, y = halves
        upper = jnp.where(low, x, roll(y, HALF))
        lower = jnp.where(low, roll(x, HALF), y)
        att_t[h * HD : (h + 1) * HD, :] = jnp.concatenate(
            [upper, lower[: HD - OUT_ROWS]], axis=0
        )
    place = jnp.broadcast_to(place_of(slots_ref[...]), (BLK, BLK))
    row_id = lax.broadcasted_iota(jnp.int32, (BLK, BLK), 0)
    hot = jnp.where(place == row_id, 1.0, 0.0).T.astype(jnp.bfloat16)
    rows = lax.dot_general(
        hot,
        att_t[...].astype(jnp.bfloat16),
        (((1,), (1,)), ((), ())),
        preferred_element_type=jnp.float32,
    ).astype(jnp.bfloat16)
    branch = jnp.dot(rows, w_ref[...], preferred_element_type=jnp.float32)
    out_ref[...] = (tokens_ref[...].astype(jnp.float32) + gate_ref[...] * branch).astype(
        jnp.bfloat16
    )


def vmem():
    return pl.BlockSpec(memory_space=pltpu.VMEM)


def body(tokens, slots, counts, shift, scale, gate, w_qkv, w_out):
    slots = slots.reshape(1, BLK)
    sent = pl.pallas_call(
        pre_kernel,
        out_shape=jax.ShapeDtypeStruct((DEVICES, IN_ROWS, BLK), jnp.bfloat16),
        in_specs=[
            pl.BlockSpec(memory_space=pltpu.SMEM),
            vmem(),
            vmem(),
            vmem(),
            vmem(),
            pl.BlockSpec(memory_space=pl.ANY),
        ],
        out_specs=vmem(),
        scratch_shapes=[
            pltpu.VMEM((W_CHUNKS, D, W_CHUNK), jnp.bfloat16),
            pltpu.VMEM((3 * D, BLK), jnp.float32),
            pltpu.SemaphoreType.DMA((W_CHUNKS,)),
        ],
        compiler_params=pltpu.CompilerParams(vmem_limit_bytes=VMEM),
        name="merge_norm_qkv",
    )(counts, slots, tokens, shift.reshape(1, D), scale.reshape(1, D), w_qkv)
    got = lax.all_to_all(sent, "patch", 0, 0, tiled=True)
    back = pl.pallas_call(
        attend_kernel,
        out_shape=jax.ShapeDtypeStruct((DEVICES, OUT_ROWS, BLK), jnp.bfloat16),
        in_specs=[vmem()],
        out_specs=vmem(),
        scratch_shapes=[
            pltpu.VMEM((144, BLK), jnp.int32),
            pltpu.SMEM((144, BLK), jnp.int32),
            pltpu.VMEM((TILES, AUG, BLK), jnp.float32),
            pltpu.VMEM((TILES, HD, BLK), jnp.float32),
            pltpu.VMEM((TILES, HD, BLK), jnp.float32),
            pltpu.VMEM((COLUMNS, BLK), jnp.bfloat16),
            pltpu.VMEM((AUG, COLUMNS), jnp.bfloat16),
            pltpu.VMEM((TILES // 2, BLK, WIDE), jnp.bfloat16),
            pltpu.VMEM((COLUMNS, WIDE), jnp.float32),
            pltpu.VMEM((COLUMNS, WIDE), jnp.bfloat16),
            pltpu.VMEM((TILES, AUG, BLK), jnp.float32),
            pltpu.SemaphoreType.DMA,
        ],
        compiler_params=pltpu.CompilerParams(vmem_limit_bytes=VMEM),
        name="attend_head",
    )(got)
    returned = lax.all_to_all(back, "patch", 0, 0, tiled=True)
    return pl.pallas_call(
        post_kernel,
        out_shape=jax.ShapeDtypeStruct((BLK, D), jnp.bfloat16),
        in_specs=[vmem()] * 5,
        out_specs=vmem(),
        scratch_shapes=[pltpu.VMEM((D, BLK), jnp.float32)],
        compiler_params=pltpu.CompilerParams(vmem_limit_bytes=VMEM),
        name="combine_project",
    )(returned, slots, tokens, gate.reshape(1, D), w_out)


def solution(mesh):
    split = ("batch", "patch")
    return jax.shard_map(
        body,
        mesh=mesh,
        in_specs=(P(split, None), P(split), P(split), P(), P(), P(), P(), P()),
        out_specs=P(split, None),
        check_vma=False,
    )
```

time: 332 us -> 103 us (0.31)
  waiting for transfers between devices: 158 us -> 13.9 us
  local copies, waits for them, and re-layouts: 69.1 us -> 4.02 us
  Pallas kernels: 0 us -> 40 us
  blocking collectives: 0 us -> 38.8 us
  matrix products: 36.7 us -> 0 us
  other arithmetic: 24.3 us -> 0 us
  starting transfers between devices: 25.4 us -> 5.54 us
  between operations: 17.1 us -> 0.69 us
    all_gather x1 -> x0, waiting for transfers between devices: 126 us -> none  [in_one_piece(): out, at, done = (lax.all_gather(both, axis, axis=dim, tiled=True), 0, [])]
    slice x5 -> x0, local copies, waits for them, and re-layouts: 49.3 us -> none  [the longest x3 49.3 us: in_one_piece(): share = out[..., at:at + column.shape[along]]]
    pallas_call x0 -> x3, Pallas kernels: none -> 40 us  [the longest x1 28.5 us: body(): pl.pallas_call(attend_kernel, out_shape=jax.ShapeDtypeStruct((DEVICES, OU...]
    all_to_all x0 -> x1, blocking collectives: none -> 38.8 us  [body(): got = lax.all_to_all(sent, 'patch', 0, 0, tiled=True)]
    dot_general x5 -> x0, matrix products: 36.7 us -> none  [the longest x1 14.7 us: attend_piece(): jnp.einsum('hqk,khe->hqe', probs.astype(jnp.bfloat16), value_heads, prefe...]
    all_to_all x3 -> x1, starting transfers between devices: 25.3 us -> 5.54 us  [body(): returned = lax.all_to_all(back, 'patch', 0, 0, tiled=True)]
    all_to_all x3 -> x1, waiting for transfers between devices: 31.9 us -> 13.9 us  [body(): returned = lax.all_to_all(back, 'patch', 0, 0, tiled=True)]
    gather x10 -> x0, local copies, waits for them, and re-layouts: 11.7 us -> none  [the longest x2 3.55 us: body(): jnp.take(live_attended, jnp.clip(back_rank.reshape(count * capacity), 0,...]
  transfers between devices with their start and end apart: 4 -> 1, of which waited for: 4 -> 1; matrix products, arithmetic and copies ran while one was open for 2% -> 1% of each run, Pallas kernels for 0% -> 0%
where the time goes in v1:
time: 103 us
  Pallas kernels  40 us (39%)
  blocking collectives  38.8 us (38%)
  waiting for transfers between devices  13.9 us (13%)
  starting transfers between devices  5.54 us (5%)
  local copies, waits for them, and re-layouts  4.02 us (4%)
    all_to_all x1, blocking collectives, body(): got = lax.all_to_all(sent, 'patch', 0, 0, tiled=True)  38.8 us
    pallas_call x1, Pallas kernels, body(): pl.pallas_call(attend_kernel, out_shape=jax.ShapeDtypeStruct((DEVICES, OU...  28.5 us
    all_to_all x1, waiting for transfers between devices, body(): returned = lax.all_to_all(back, 'patch', 0, 0, tiled=True)  13.9 us
    pallas_call x1, Pallas kernels, body(): pl.pallas_call(pre_kernel, out_shape=jax.ShapeDtypeStruct((DEVICES, IN_RO...  7.75 us
    all_to_all x1, starting transfers between devices, body(): returned = lax.all_to_all(back, 'patch', 0, 0, tiled=True)  5.54 us
    pallas_call x1, Pallas kernels, body(): pl.pallas_call(post_kernel, out_shape=jax.ShapeDtypeStruct((BLK, D), jnp....  3.71 us
  transfers between devices with their start and end apart: 1, of which 1 were waited for; matrix products, arithmetic and copies ran while one was open for 1% of the time, Pallas kernels for 0%

profile of v1, /device:TPU:0, one launch (start us, length us, event | category | flops | bytes accessed | tf_op | source)
XLA Modules:
  0.0 103.0 jit_solution(5705149587491269029)
XLA Ops:
  0.0 1.3 %reshape.13.shift_ref = f32[1,1152]{1,0:T(1,128)} reshape(f32[1152]{0:T(1024)} %param.11) | data formatting | bytes 9216 | tf_op jit(solution)/shard_map/reshape | solution.py:275
  1.3 1.3 %reshape.14.scale_ref = f32[1,1152]{1,0:T(1,128)} reshape(f32[1152]{0:T(1024)} %param.12) | data formatting | bytes 9216 | tf_op jit(solution)/shard_map/reshape | solution.py:275
  3.2 7.8 %merge_norm_qkv.1 = bf16[64,112,128]{2,1,0:T(8,128)(2,1)} custom-call(s32[1]{0:T(128)S(6)} %copy.9.counts_ref, s32[1,128]{1,0:T(1,128)} %bitcast.1, bf16[128,1152]{1,0:T(8,128)(2,1)} %tokens_ref.3, f32[1,1152]{1,0:T(1,128)} %reshape.13.shift_ref, f32[1,1152]{1,0:T(1,128)} %reshape.14.scale_ref, bf16[1152,3456]{1,0:T(8,128)(2,1)} %w_ref.2), custom_call_target="tpu_custom_call" | custom-call | tf_op jit(solution)/shard_map/merge_norm_qkv/pallas_call | solution.py:256
  11.0 38.8 %all_to_all.10.got_ref = bf16[64,112,128]{2,1,0:T(8,128)(2,1)} all-to-all(bf16[64,112,128]{2,1,0:T(8,128)(2,1)} %merge_norm_qkv.1), channel_id=1, replica_groups=mesh['patch'=64,'batch'=2] {'patch'}, dimensions={0} | all-to-all | bytes 3670016 | tf_op jit(solution)/shard_map/all_to_all | solution.py:276
  49.8 0.0 copy-start.1
  49.8 28.5 %attend_head.1 = bf16[64,40,128]{2,1,0:T(8,128)(2,1)} custom-call(bf16[64,112,128]{2,1,0:T(8,128)(2,1)} %all_to_all.10.got_ref), custom_call_target="tpu_custom_call" | custom-call | tf_op jit(solution)/shard_map/attend_head/pallas_call | solution.py:277
  78.3 5.5 %all-to-all-start.1 = ((bf16[64,40,128]{2,1,0:T(8,128)(2,1)}), bf16[64,40,128]{2,1,0:T(8,128)(2,1)S(1)}, u32[]{:S(2)}, u32[]{:S(2)}) async-start(bf16[64,40,128]{2,1,0:T(8,128)(2,1)} %attend_head.1), calls=%async_computation.1 | async-start | bytes 1310720 | tf_op jit(solution)/shard_map/all_to_all | solution.py:299
  83.9 0.0 copy-done.1
  83.9 0.6 reshape.15.gate_ref
  84.5 13.9 %all-to-all-done.1.got_ref = bf16[64,40,128]{2,1,0:T(8,128)(2,1)S(1)} async-done(((bf16[64,40,128]{2,1,0:T(8,128)(2,1)}), bf16[64,40,128]{2,1,0:T(8,128)(2,1)S(1)}, u32[]{:S(2)}, u32[]{:S(2)}) %all-to-all-start.1) | async-done | bytes 655392 | tf_op jit(solution)/shard_map/all_to_all | solution.py:299
  98.4 0.0 copy-start
  98.4 0.8 copy-done
  99.3 3.7 %combine_project.1 = bf16[128,1152]{1,0:T(8,128)(2,1)} custom-call(bf16[64,40,128]{2,1,0:T(8,128)(2,1)} %copy-done, s32[1,128]{1,0:T(1,128)} %bitcast.2, bf16[128,1152]{1,0:T(8,128)(2,1)} %tokens_ref.3, f32[1,1152]{1,0:T(1,128)} %reshape.15.gate_ref, bf16[1152,1152]{1,0:T(8,128)(2,1)} %w_ref.3), custom_call_target="tpu_custom_call" | custom-call | tf_op jit(solution)/shard_map/combine_project/pallas_call | solution.py:300
Async XLA Ops:
  49.8 34.1 %copy-start.1 = (f32[1152]{0:T(1024)S(1)}, f32[1152]{0:T(1024)}, u32[]{:S(2)}) copy-start(f32[1152]{0:T(1024)} %param.13) | copy-start | bytes 13828
  78.3 20.1 %all-to-all-start.1 = ((bf16[64,40,128]{2,1,0:T(8,128)(2,1)}), bf16[64,40,128]{2,1,0:T(8,128)(2,1)S(1)}, u32[]{:S(2)}, u32[]{:S(2)}) async-start(bf16[64,40,128]{2,1,0:T(8,128)(2,1)} %attend_head.1), calls=%async_computation.1 | async-start | bytes 1310720 | tf_op jit(solution)/shard_map/all_to_all | solution.py:299
  98.4 0.8 copy-start

commit v2 on v1

--- a/solution.py
+++ b/solution.py
@@ -18,7 +18,9 @@
 AUG = 80
 TILES = 22
 WIDE = 2 * BLK
-COLUMNS = TILES * BLK
+COLUMNS = (TILES - 1) * BLK
+Q_ROWS = 288
+Q_TILES = 9
 W_CHUNK = 384
 W_CHUNKS = 3 * D // W_CHUNK
 VMEM = 56 * 1024 * 1024
@@ -36,7 +38,7 @@
 
 
 def pre_kernel(
-    counts_ref, slots_ref, tokens_ref, shift_ref, scale_ref, w_ref, out_ref, w_buf, qkv_t, sems
+    slots_ref, tokens_ref, shift_ref, scale_ref, w_ref, out_ref, w_buf, qkv_t, sems
 ):
     copies = [
         pltpu.make_async_copy(
@@ -68,8 +70,10 @@
     members_row = jnp.sum(hot.T, axis=0, keepdims=True)
     low = lax.broadcasted_iota(jnp.int32, (1, BLK), 1) < HALF
     line = lax.broadcasted_iota(jnp.int32, (8, BLK), 0)
-    count = counts_ref[0]
-    live = [((count + 1) >> 1).astype(jnp.float32), (count >> 1).astype(jnp.float32)]
+    alive = jnp.where(members_row > 0.0, 1.0, 0.0)
+    live = [
+        jnp.sum(jnp.where(low == even, alive, 0.0), axis=1, keepdims=True) for even in (True, False)
+    ]
     sizes_of = [roll(jnp.broadcast_to(members_row, (8, BLK)), HALF)]
     sizes_of.append(jnp.broadcast_to(members_row, (8, BLK)))
     sizes = [
@@ -113,8 +117,11 @@
     keys,
     vals,
     queries,
-    scores,
-    probs,
+    scores_a,
+    scores_b,
+    top_a,
+    top_b,
+    done,
     done_t,
     sem,
 ):
@@ -159,49 +166,92 @@
         put(q_t, q_tile, 64, HD, roll(message[104:], q_off), keep_q)
         return 0
 
-    lax.fori_loop(0, DEVICES, pack, 0, unroll=2)
+    lax.fori_loop(0, DEVICES, pack, 0, unroll=8)
 
     total = offs[64, HALF]
     line8 = lax.broadcasted_iota(jnp.int32, (8, BLK), 0)
     zeros = jnp.zeros((BLK - AUG, BLK), jnp.float32)
     ones2 = jnp.where(line8 < 2, 1.0, 0.0)
     ones1 = jnp.where(line8 < 1, 1.0, 0.0)
-    written = TILES - 1
-    for t in range(TILES):
-        if t < written:
-            members = jnp.broadcast_to(k_t[t, HD : HD + 1, :], (8, BLK))
-            bias = jnp.log(jnp.maximum(members, 1.0)) * (1.0 / INVERSE)
-            bias = jnp.where(lane + t * BLK < total, bias, -1e30)
-            high = bias.astype(jnp.bfloat16).astype(jnp.float32)
-            rest = jnp.where(line8 == 0, high, jnp.where(line8 == 1, bias - high, 0.0))
-            k_tile, v_tile, q_tile = k_t[t, :HD, :], v_t[t, :HD, :], q_t[t, :HD, :]
-        else:
-            rest = jnp.where(line8 == 0, -1e30, 0.0)
-            k_tile = v_tile = q_tile = jnp.zeros((HD, BLK), jnp.float32)
+    for t in range(TILES - 1):
+        members = jnp.broadcast_to(k_t[t, HD : HD + 1, :], (8, BLK))
+        bias = jnp.log(jnp.maximum(members, 1.0)) * (1.0 / INVERSE)
+        bias = jnp.where(lane + t * BLK < total, bias, -1e30)
+        high = bias.astype(jnp.bfloat16).astype(jnp.float32)
+        rest = jnp.where(line8 == 0, high, jnp.where(line8 == 1, bias - high, 0.0))
+        k_tile, v_tile, q_tile = k_t[t, :HD, :], v_t[t, :HD, :], q_t[t, :HD, :]
         cols = slice(t * BLK, (t + 1) * BLK)
-        keys[cols, :] = jnp.concatenate([k_tile, rest, zeros], axis=0).T.astype(jnp.bfloat16)
-        vals[:, cols] = jnp.concatenate([v_tile, ones1], axis=0).astype(jnp.bfloat16)
-        queries[t // 2, :, (t % 2) * BLK : (t % 2 + 1) * BLK] = jnp.concatenate(
-            [q_tile, ones2, zeros], axis=0
-        ).astype(jnp.bfloat16)
-
-    def attend(i, _):
-        s = jnp.dot(keys[...], queries[i], preferred_element_type=jnp.float32)
-        scores[...] = s
-        top = jnp.max(s, axis=0, keepdims=True)
-        probs[...] = jnp.exp2((scores[...] - top) * (INVERSE * LOG2E)).astype(jnp.bfloat16)
-        o = jnp.dot(vals[...], probs[...], preferred_element_type=jnp.float32)
-        mass = o[HD : HD + 1]
-        lse = jnp.broadcast_to(top * INVERSE + jnp.log(mass), (8, WIDE))
-        high = lse.astype(jnp.bfloat16).astype(jnp.float32)
-        line = lax.broadcasted_iota(jnp.int32, (8, WIDE), 0)
-        stats = jnp.where(line == 0, high, jnp.where(line == 1, lse - high, 0.0))
-        o = jnp.concatenate([o[:HD] * (1.0 / mass), stats], axis=0)
-        done_t[2 * i] = o[:, :BLK]
-        done_t[2 * i + 1] = o[:, BLK:]
+        keys[:, cols] = jnp.concatenate([k_tile, rest, zeros], axis=0).astype(jnp.bfloat16)
+        vals[cols, :] = jnp.concatenate([v_tile, ones1, zeros], axis=0).T.astype(jnp.bfloat16)
+        queries[cols, :] = jnp.concatenate([q_tile, ones2, zeros], axis=0).T.astype(jnp.bfloat16)
+
+    chunks = [slice(at, min(at + WIDE, COLUMNS)) for at in range(0, COLUMNS, WIDE)]
+
+    def rows_of(i):
+        return pl.ds(pl.multiple_of(i * Q_ROWS, 16), Q_ROWS)
+
+    def fold(s, best):
+        for t in range(s.shape[1] // BLK):
+            part = s[:, t * BLK : (t + 1) * BLK]
+            best = part if best is None else jnp.maximum(best, part)
+        return best
+
+    def step(i, scores, top, ahead_scores, ahead_top):
+        best = None
+        o = None
+        q = queries[rows_of(i + 1), :] if ahead_scores is not None else None
+        for c in chunks:
+            if ahead_scores is not None:
+                s = jnp.dot(q, keys[:, c], preferred_element_type=jnp.float32)
+                ahead_scores[:, c] = s
+                best = fold(s, best)
+            if scores is not None:
+                n = (c.stop - c.start) // BLK
+                p = [
+                    jnp.exp2(
+                        (scores[:, c.start + t * BLK : c.start + (t + 1) * BLK] - top[...])
+                        * (INVERSE * LOG2E)
+                    ).astype(jnp.bfloat16)
+                    for t in range(n)
+                ]
+                p = jnp.concatenate(p, axis=1)
+                part = jnp.dot(p, vals[c, :], preferred_element_type=jnp.float32)
+                o = part if o is None else o + part
+        if ahead_scores is not None:
+            ahead_top[...] = jnp.broadcast_to(
+                jnp.max(best, axis=1, keepdims=True), (Q_ROWS, BLK)
+            )
+        if scores is not None:
+            mass = jnp.broadcast_to(o[:, HD : HD + 1], (Q_ROWS, BLK))
+            lse = top[...] * INVERSE + jnp.log(mass)
+            high = lse.astype(jnp.bfloat16).astype(jnp.float32)
+            done[rows_of(i), :] = jnp.where(
+                lane < HD, o / mass, jnp.where(lane == HD, high, lse - high)
+            )
+
+    def two(i, _):
+        step(2 * i, scores_a, top_a, scores_b, top_b)
+        step(2 * i + 1, scores_b, top_b, scores_a, top_a)
         return 0
 
-    lax.fori_loop(0, TILES // 2, attend, 0)
+    step(-1, None, None, scores_a, top_a)
+    pairs = (Q_TILES - 1) // 2
+    lax.fori_loop(0, pairs, two, 0)
+    if Q_TILES % 2 == 0:
+        step(Q_TILES - 2, scores_a, top_a, scores_b, top_b)
+        step(Q_TILES - 1, scores_b, top_b, None, None)
+    else:
+        step(Q_TILES - 1, scores_a, top_a, None, None)
+
+    for t in range(TILES - 1):
+        last = min((t + 1) * BLK, Q_TILES * Q_ROWS)
+        tile = done[t * BLK : last, :]
+        if last < (t + 1) * BLK:
+            tile = jnp.concatenate(
+                [tile, jnp.zeros(((t + 1) * BLK - last, BLK), jnp.float32)], axis=0
+            )
+        done_t[t] = tile.T[:AUG]
+    done_t[TILES - 1] = jnp.zeros((AUG, BLK), jnp.float32)
 
     def unpack(b, _):
         at = offs[72 + b, HALF]
@@ -212,10 +262,12 @@
         out_ref[b] = jnp.where(low, first, second).astype(jnp.bfloat16)
         return 0
 
-    lax.fori_loop(0, DEVICES, unpack, 0, unroll=2)
-
-
-def post_kernel(got_ref, slots_ref, tokens_ref, gate_ref, w_ref, out_ref, att_t):
+    lax.fori_loop(0, DEVICES, unpack, 0, unroll=8)
+
+
+def post_kernel(got_ref, slots_ref, tokens_ref, gate_ref, w_ref, out_ref, att_t, w_buf, sem):
+    copy = pltpu.make_async_copy(w_ref, w_buf, sem)
+    copy.start()
     low = lax.broadcasted_iota(jnp.int32, (1, BLK), 1) < HALF
     for h in range(HEADS):
         halves = []
@@ -241,7 +293,8 @@
         (((1,), (1,)), ((), ())),
         preferred_element_type=jnp.float32,
     ).astype(jnp.bfloat16)
-    branch = jnp.dot(rows, w_ref[...], preferred_element_type=jnp.float32)
+    copy.wait()
+    branch = jnp.dot(rows, w_buf[...], preferred_element_type=jnp.float32)
     out_ref[...] = (tokens_ref[...].astype(jnp.float32) + gate_ref[...] * branch).astype(
         jnp.bfloat16
     )
@@ -251,13 +304,11 @@
     return pl.BlockSpec(memory_space=pltpu.VMEM)
 
 
-def body(tokens, slots, counts, shift, scale, gate, w_qkv, w_out):
-    slots = slots.reshape(1, BLK)
-    sent = pl.pallas_call(
+def pre(slots, tokens, shift, scale, w_qkv):
+    return pl.pallas_call(
         pre_kernel,
         out_shape=jax.ShapeDtypeStruct((DEVICES, IN_ROWS, BLK), jnp.bfloat16),
         in_specs=[
-            pl.BlockSpec(memory_space=pltpu.SMEM),
             vmem(),
             vmem(),
             vmem(),
@@ -272,9 +323,11 @@
         ],
         compiler_params=pltpu.CompilerParams(vmem_limit_bytes=VMEM),
         name="merge_norm_qkv",
-    )(counts, slots, tokens, shift.reshape(1, D), scale.reshape(1, D), w_qkv)
-    got = lax.all_to_all(sent, "patch", 0, 0, tiled=True)
-    back = pl.pallas_call(
+    )(slots, tokens, shift, scale, w_qkv)
+
+
+def attend(got):
+    return pl.pallas_call(
         attend_kernel,
         out_shape=jax.ShapeDtypeStruct((DEVICES, OUT_ROWS, BLK), jnp.bfloat16),
         in_specs=[vmem()],
@@ -285,27 +338,44 @@
             pltpu.VMEM((TILES, AUG, BLK), jnp.float32),
             pltpu.VMEM((TILES, HD, BLK), jnp.float32),
             pltpu.VMEM((TILES, HD, BLK), jnp.float32),
+            pltpu.VMEM((BLK, COLUMNS), jnp.bfloat16),
             pltpu.VMEM((COLUMNS, BLK), jnp.bfloat16),
-            pltpu.VMEM((AUG, COLUMNS), jnp.bfloat16),
-            pltpu.VMEM((TILES // 2, BLK, WIDE), jnp.bfloat16),
-            pltpu.VMEM((COLUMNS, WIDE), jnp.float32),
-            pltpu.VMEM((COLUMNS, WIDE), jnp.bfloat16),
+            pltpu.VMEM((COLUMNS, BLK), jnp.bfloat16),
+            pltpu.VMEM((Q_ROWS, COLUMNS), jnp.float32),
+            pltpu.VMEM((Q_ROWS, COLUMNS), jnp.float32),
+            pltpu.VMEM((Q_ROWS, BLK), jnp.float32),
+            pltpu.VMEM((Q_ROWS, BLK), jnp.float32),
+            pltpu.VMEM((Q_ROWS * Q_TILES, BLK), jnp.float32),
             pltpu.VMEM((TILES, AUG, BLK), jnp.float32),
             pltpu.SemaphoreType.DMA,
         ],
         compiler_params=pltpu.CompilerParams(vmem_limit_bytes=VMEM),
         name="attend_head",
     )(got)
-    returned = lax.all_to_all(back, "patch", 0, 0, tiled=True)
+
+
+def post(returned, slots, tokens, gate, w_out):
     return pl.pallas_call(
         post_kernel,
         out_shape=jax.ShapeDtypeStruct((BLK, D), jnp.bfloat16),
-        in_specs=[vmem()] * 5,
+        in_specs=[vmem()] * 4 + [pl.BlockSpec(memory_space=pl.ANY)],
         out_specs=vmem(),
-        scratch_shapes=[pltpu.VMEM((D, BLK), jnp.float32)],
+        scratch_shapes=[
+            pltpu.VMEM((D, BLK), jnp.float32),
+            pltpu.VMEM((D, D), jnp.bfloat16),
+            pltpu.SemaphoreType.DMA,
+        ],
         compiler_params=pltpu.CompilerParams(vmem_limit_bytes=VMEM),
         name="combine_project",
-    )(returned, slots, tokens, gate.reshape(1, D), w_out)
+    )(returned, slots, tokens, gate, w_out)
+
+
+def body(tokens, slots, counts, shift, scale, gate, w_qkv, w_out):
+    sent = pre(slots, tokens, shift, scale, w_qkv)
+    got = lax.all_to_all(sent, "patch", 0, 0, tiled=True)
+    back = attend(got)
+    returned = lax.all_to_all(back, "patch", 0, 0, tiled=True)
+    return post(returned, slots, tokens, gate, w_out)
 
 
 def solution(mesh):

time: 103 us -> 88.2 us (0.86)
  blocking collectives: 38.8 us -> 59 us
  waiting for transfers between devices: 13.9 us -> 0 us
  Pallas kernels: 40 us -> 28.8 us
  starting transfers between devices: 5.54 us -> 0 us
  local copies, waits for them, and re-layouts: 4.02 us -> 0 us
    all_to_all x0 -> x1, blocking collectives: none -> 20.2 us  [body(): returned = lax.all_to_all(back, 'patch', 0, 0, tiled=True)]
    all_to_all x1 -> x0, waiting for transfers between devices: 13.9 us -> none  [body(): returned = lax.all_to_all(back, 'patch', 0, 0, tiled=True)]
    pallas_call x3, Pallas kernels: 40 us -> 28.8 us  [the longest x1 16.8 us: attend(): pl.pallas_call(attend_kernel, out_shape=jax.ShapeDtypeStruct((DEVICES, OU...]
    all_to_all x1 -> x0, starting transfers between devices: 5.54 us -> none  [body(): returned = lax.all_to_all(back, 'patch', 0, 0, tiled=True)]
    reshape x3 -> x0, local copies, waits for them, and re-layouts: 3.18 us -> none  [the longest x1 1.29 us: body(): scale.reshape(1, D)]
  transfers between devices with their start and end apart: 1 -> 0, of which waited for: 1 -> 0; matrix products, arithmetic and copies ran while one was open for 1% -> 0% of each run, Pallas kernels for 0% -> 0%
where the time goes in v2:
time: 88.2 us; the launch traced here: 87.8 us
  blocking collectives  59 us (67%)
  Pallas kernels  28.8 us (33%)
    all_to_all x1, blocking collectives, body(): got = lax.all_to_all(sent, 'patch', 0, 0, tiled=True)  38.8 us
    all_to_all x1, blocking collectives, body(): returned = lax.all_to_all(back, 'patch', 0, 0, tiled=True)  20.2 us
    pallas_call x1, Pallas kernels, attend(): pl.pallas_call(attend_kernel, out_shape=jax.ShapeDtypeStruct((DEVICES, OU...  16.8 us
    pallas_call x1, Pallas kernels, pre(): pl.pallas_call(pre_kernel, out_shape=jax.ShapeDtypeStruct((DEVICES, IN_RO...  7.73 us
    pallas_call x1, Pallas kernels, post(): pl.pallas_call(post_kernel, out_shape=jax.ShapeDtypeStruct((BLK, D), jnp....  4.26 us

profile of v2, /device:TPU:0, one launch (start us, length us, event | category | flops | bytes accessed | tf_op | source)
XLA Modules:
  0.0 87.8 jit_solution(1327005534801670403)
XLA Ops:
  0.0 7.7 %merge_norm_qkv.1 = bf16[64,112,128]{2,1,0:T(8,128)(2,1)} custom-call(s32[128]{0:T(128)} %slots_ref.3, bf16[128,1152]{1,0:T(8,128)(2,1)} %tokens_ref.3, f32[1152]{0:T(1024)} %shift_ref.1, f32[1152]{0:T(1024)} %scale_ref.1, bf16[1152,3456]{1,0:T(8,128)(2,1)} %w_ref.2), custom_call_target="tpu_custom_call" | custom-call | tf_op jit(solution)/shard_map/merge_norm_qkv/pallas_call | solution.py:308
  7.7 38.8 %all_to_all.10.got_ref = bf16[64,112,128]{2,1,0:T(8,128)(2,1)} all-to-all(bf16[64,112,128]{2,1,0:T(8,128)(2,1)} %merge_norm_qkv.1), channel_id=1, replica_groups=mesh['patch'=64,'batch'=2] {'patch'}, dimensions={0} | all-to-all | bytes 3670016 | tf_op jit(solution)/shard_map/all_to_all | solution.py:375
  46.5 16.8 %attend_head.1 = bf16[64,40,128]{2,1,0:T(8,128)(2,1)} custom-call(bf16[64,112,128]{2,1,0:T(8,128)(2,1)} %all_to_all.10.got_ref), custom_call_target="tpu_custom_call" | custom-call | tf_op jit(solution)/shard_map/attend_head/pallas_call | solution.py:330
  63.4 20.2 %all_to_all.11.got_ref = bf16[64,40,128]{2,1,0:T(8,128)(2,1)} all-to-all(bf16[64,40,128]{2,1,0:T(8,128)(2,1)} %attend_head.1), channel_id=1, replica_groups=mesh['patch'=64,'batch'=2] {'patch'}, dimensions={0} | all-to-all | bytes 1310720 | tf_op jit(solution)/shard_map/all_to_all | solution.py:377
  83.5 4.3 %combine_project.1 = bf16[128,1152]{1,0:T(8,128)(2,1)} custom-call(bf16[64,40,128]{2,1,0:T(8,128)(2,1)} %all_to_all.11.got_ref, s32[128]{0:T(128)} %slots_ref.3, bf16[128,1152]{1,0:T(8,128)(2,1)} %tokens_ref.3, f32[1152]{0:T(1024)} %gate_ref.1, bf16[1152,1152]{1,0:T(8,128)(2,1)} %w_ref.3), custom_call_target="tpu_custom_call" | custom-call | tf_op jit(solution)/shard_map/combine_project/pallas_call | solution.py:358

commit v3 on v2

--- a/solution.py
+++ b/solution.py
@@ -17,12 +17,12 @@
 OUT_ROWS = 40
 AUG = 80
 TILES = 22
-WIDE = 2 * BLK
+CHUNK = 2 * BLK
 COLUMNS = (TILES - 1) * BLK
-Q_ROWS = 288
-Q_TILES = 9
-W_CHUNK = 384
-W_CHUNKS = 3 * D // W_CHUNK
+Q_ROWS = 656
+PIECES = 4
+Q_TILES = 4
+EARLY = 64
 VMEM = 56 * 1024 * 1024
 
 INVERSE = 1.0 / HD**0.5
@@ -38,35 +38,48 @@
 
 
 def pre_kernel(
-    slots_ref, tokens_ref, shift_ref, scale_ref, w_ref, out_ref, w_buf, qkv_t, sems
+    slots_ref,
+    tokens_ref,
+    shift_ref,
+    scale_ref,
+    w_ref,
+    out_ref,
+    slots_buf,
+    tok_buf,
+    shift_buf,
+    scale_buf,
+    w_buf,
+    qkv_t,
+    messages,
+    in_sems,
+    w_sems,
+    out_sems,
 ):
-    copies = [
-        pltpu.make_async_copy(
-            w_ref.at[:, pl.ds(c * W_CHUNK, W_CHUNK)], w_buf.at[c], sems.at[c]
+    small = [
+        pltpu.make_async_copy(src, dst, in_sems.at[i])
+        for i, (src, dst) in enumerate(
+            [
+                (slots_ref, slots_buf),
+                (tokens_ref, tok_buf),
+                (shift_ref, shift_buf),
+                (scale_ref, scale_buf),
+            ]
         )
-        for c in range(W_CHUNKS)
-    ]
-    for copy in copies:
+    ]
+    for copy in small:
         copy.start()
-    place = jnp.broadcast_to(place_of(slots_ref[...]), (BLK, BLK))
+    large = [
+        pltpu.make_async_copy(w_ref.at[:, pl.ds(part * D, D)], w_buf.at[part], w_sems.at[part])
+        for part in (1, 2, 0)
+    ]
+    for copy in large:
+        copy.start()
+
+    small[0].wait()
+    place = jnp.broadcast_to(place_of(slots_buf[...]), (BLK, BLK))
     row_id = lax.broadcasted_iota(jnp.int32, (BLK, BLK), 0)
     hot = jnp.where(place == row_id, 1.0, 0.0)
     members = jnp.sum(hot, axis=1, keepdims=True)
-    sums = jnp.dot(hot.astype(jnp.bfloat16), tokens_ref[...], preferred_element_type=jnp.float32)
-    values = (sums / jnp.maximum(members, 1.0)).astype(jnp.bfloat16).astype(jnp.float32)
-    center = jnp.mean(values, axis=-1, keepdims=True)
-    off = values - center
-    spread = jnp.mean(off * off, axis=-1, keepdims=True)
-    normed = (off * lax.rsqrt(spread + 1e-06) * (1.0 + scale_ref[...]) + shift_ref[...]).astype(
-        jnp.bfloat16
-    )
-    for c in range(W_CHUNKS):
-        copies[c].wait()
-        part = jnp.dot(normed, w_buf[c], preferred_element_type=jnp.float32)
-        for t in range(W_CHUNK // BLK):
-            at = c * W_CHUNK + t * BLK
-            qkv_t[at : at + BLK, :] = part[:, t * BLK : (t + 1) * BLK].T
-
     members_row = jnp.sum(hot.T, axis=0, keepdims=True)
     low = lax.broadcasted_iota(jnp.int32, (1, BLK), 1) < HALF
     line = lax.broadcasted_iota(jnp.int32, (8, BLK), 0)
@@ -87,12 +100,45 @@
         ]
         for a in range(2)
     ]
+
+    for copy in small[1:]:
+        copy.wait()
+    sums = jnp.dot(hot.astype(jnp.bfloat16), tok_buf[...], preferred_element_type=jnp.float32)
+    values = (sums / jnp.maximum(members, 1.0)).astype(jnp.bfloat16).astype(jnp.float32)
+    center = jnp.mean(values, axis=-1, keepdims=True)
+    off = values - center
+    spread = jnp.mean(off * off, axis=-1, keepdims=True)
+    normed = (off * lax.rsqrt(spread + 1e-06) * (1.0 + scale_buf[...]) + shift_buf[...]).astype(
+        jnp.bfloat16
+    )
+
+    def project(part):
+        out = jnp.dot(normed, w_buf[part], preferred_element_type=jnp.float32)
+        for t in range(D // BLK):
+            qkv_t[part, t * BLK : (t + 1) * BLK, :] = out[:, t * BLK : (t + 1) * BLK].T
+
+    large[0].wait()
+    project(1)
+    large[1].wait()
+    project(2)
+    early = []
     for h in range(HEADS):
-        q = qkv_t[h * HD : (h + 1) * HD, :]
-        k = qkv_t[D + h * HD : D + (h + 1) * HD, :]
-        v = qkv_t[2 * D + h * HD : 2 * D + (h + 1) * HD, :]
-        q_roll, k_roll, v_roll = roll(q, HALF), roll(k, HALF), roll(v, HALF)
-        kv = [jnp.where(low, k, v_roll), jnp.where(low, k_roll, v)]
+        k = qkv_t[1, h * HD : (h + 1) * HD, :]
+        v = qkv_t[2, h * HD : (h + 1) * HD, :]
+        kv = [jnp.where(low, k, roll(v, HALF)), jnp.where(low, roll(k, HALF), v)]
+        early.append([x[EARLY:] for x in kv])
+        for a in range(2):
+            for b in range(2):
+                messages[h * GROUPS + 2 * a + b, :EARLY, :] = kv[b][:EARLY].astype(jnp.bfloat16)
+    first = pltpu.make_async_copy(
+        messages.at[:, pl.ds(0, EARLY)], out_ref.at[:, pl.ds(0, EARLY)], out_sems.at[0]
+    )
+    first.start()
+    large[2].wait()
+    project(0)
+    for h in range(HEADS):
+        q = qkv_t[0, h * HD : (h + 1) * HD, :]
+        q_roll = roll(q, HALF)
         q_pair = [
             jnp.where(low, q[:32], q_roll[32:64]),
             jnp.where(low, q_roll[:32], q[32:64]),
@@ -101,14 +147,25 @@
         for a in range(2):
             for b in range(2):
                 last = jnp.where(low, q_last[a], sizes[a][b])
-                out_ref[h * GROUPS + 2 * a + b] = jnp.concatenate(
-                    [kv[b], q_pair[a], last], axis=0
+                messages[h * GROUPS + 2 * a + b, EARLY:, :] = jnp.concatenate(
+                    [early[h][b], q_pair[a], last], axis=0
                 ).astype(jnp.bfloat16)
+    second = pltpu.make_async_copy(
+        messages.at[:, pl.ds(EARLY, IN_ROWS - EARLY)],
+        out_ref.at[:, pl.ds(EARLY, IN_ROWS - EARLY)],
+        out_sems.at[1],
+    )
+    second.start()
+    first.wait()
+    second.wait()
 
 
 def attend_kernel(
     got_ref,
     out_ref,
+    tail,
+    got,
+    out,
     offs_v,
     offs,
     k_t,
@@ -124,20 +181,37 @@
     done,
     done_t,
     sem,
+    tail_sem,
+    got_sems,
+    out_sems,
 ):
+    each = DEVICES // PIECES
+    pieces = [pl.ds(i * each, each) for i in range(PIECES)]
+    tail_copy = pltpu.make_async_copy(
+        got_ref.at[:, pl.ds(IN_ROWS - 16, 16)], tail, tail_sem
+    )
+    tail_copy.start()
+    got_copies = [
+        pltpu.make_async_copy(got_ref.at[p], got.at[p], got_sems.at[i])
+        for i, p in enumerate(pieces)
+    ]
+    for copy in got_copies:
+        copy.start()
     lane = lax.broadcasted_iota(jnp.int32, (1, BLK), 1)
     low = lane < HALF
 
-    row = lax.broadcasted_iota(jnp.int32, (144, DEVICES * 16), 0)
-    col = lax.broadcasted_iota(jnp.int32, (144, DEVICES * 16), 1)
-    is_q = row >= 72
-    index = jnp.where(is_q, row - 72, row)
-    line = jnp.where(is_q, 10, 9)
-    before = ((col & 15) == line) & ((col >> 4) < index)
-    tail = got_ref[:, IN_ROWS - 16 :, :].reshape(DEVICES * 16, BLK)
-    offs_v[...] = jnp.dot(
-        jnp.where(before, 1.0, 0.0).astype(jnp.bfloat16), tail, preferred_element_type=jnp.float32
-    ).astype(jnp.int32)
+    row = lax.broadcasted_iota(jnp.int32, (BLK, DEVICES * 16), 0)
+    col = lax.broadcasted_iota(jnp.int32, (BLK, DEVICES * 16), 1)
+    tail_copy.wait()
+    last_rows = tail[...].reshape(DEVICES * 16, BLK)
+    for x in range(2):
+        before = (col < row * 16) & ((col & 15) == 9 + x)
+        sums = jnp.dot(
+            jnp.where(before, 1.0, 0.0).astype(jnp.bfloat16),
+            last_rows,
+            preferred_element_type=jnp.float32,
+        )
+        offs_v[8 * x : 8 * x + 8, :] = sums.T[HALF : HALF + 8].astype(jnp.int32)
     copy = pltpu.make_async_copy(offs_v, offs, sem)
     copy.start()
     copy.wait()
@@ -151,11 +225,11 @@
     q_t[0] = jnp.zeros_like(q_t[0])
 
     def pack(b, _):
-        k_at = offs[b, HALF]
-        q_at = offs[72 + b, HALF]
+        k_at = offs[0, b]
+        q_at = offs[8, b]
         k_tile, k_off = k_at >> 7, k_at & 127
         q_tile, q_off = q_at >> 7, q_at & 127
-        message = got_ref[b].astype(jnp.float32)
+        message = got[b].astype(jnp.float32)
         keep_k, keep_q = lane >= k_off, lane >= q_off
         k_over, q_over = (k_off + HALF) & 127, (q_off + HALF) & 127
         put(k_t, k_tile, 0, HD, roll(message[:HD], k_off), keep_k)
@@ -166,9 +240,11 @@
         put(q_t, q_tile, 64, HD, roll(message[104:], q_off), keep_q)
         return 0
 
-    lax.fori_loop(0, DEVICES, pack, 0, unroll=8)
-
-    total = offs[64, HALF]
+    for i in range(PIECES):
+        got_copies[i].wait()
+        lax.fori_loop(i * each, (i + 1) * each, pack, 0, unroll=each)
+
+    total = offs[0, DEVICES]
     line8 = lax.broadcasted_iota(jnp.int32, (8, BLK), 0)
     zeros = jnp.zeros((BLK - AUG, BLK), jnp.float32)
     ones2 = jnp.where(line8 < 2, 1.0, 0.0)
@@ -185,7 +261,7 @@
         vals[cols, :] = jnp.concatenate([v_tile, ones1, zeros], axis=0).T.astype(jnp.bfloat16)
         queries[cols, :] = jnp.concatenate([q_tile, ones2, zeros], axis=0).T.astype(jnp.bfloat16)
 
-    chunks = [slice(at, min(at + WIDE, COLUMNS)) for at in range(0, COLUMNS, WIDE)]
+    chunks = [slice(at, min(at + CHUNK, COLUMNS)) for at in range(0, COLUMNS, CHUNK)]
 
     def rows_of(i):
         return pl.ds(pl.multiple_of(i * Q_ROWS, 16), Q_ROWS)
@@ -254,25 +330,70 @@
     done_t[TILES - 1] = jnp.zeros((AUG, BLK), jnp.float32)
 
     def unpack(b, _):
-        at = offs[72 + b, HALF]
+        at = offs[8, b]
         tile, off = at >> 7, at & 127
         both = jnp.where(lane >= off, done_t[tile], done_t[tile + 1])
         first = roll(both[:OUT_ROWS], (BLK - off) & 127)
         second = roll(both[OUT_ROWS:], (BLK + HALF - off) & 127)
-        out_ref[b] = jnp.where(low, first, second).astype(jnp.bfloat16)
+        out[b] = jnp.where(low, first, second).astype(jnp.bfloat16)
         return 0
 
-    lax.fori_loop(0, DEVICES, unpack, 0, unroll=8)
-
-
-def post_kernel(got_ref, slots_ref, tokens_ref, gate_ref, w_ref, out_ref, att_t, w_buf, sem):
-    copy = pltpu.make_async_copy(w_ref, w_buf, sem)
-    copy.start()
+    out_copies = []
+    for i, p in enumerate(pieces):
+        lax.fori_loop(i * each, (i + 1) * each, unpack, 0, unroll=each)
+        out_copies.append(pltpu.make_async_copy(out.at[p], out_ref.at[p], out_sems.at[i]))
+        out_copies[i].start()
+    for copy in out_copies:
+        copy.wait()
+
+
+def post_kernel(
+    got_ref,
+    slots_ref,
+    tokens_ref,
+    gate_ref,
+    w_ref,
+    out_ref,
+    got,
+    slots_buf,
+    tok_buf,
+    gate_buf,
+    w_buf,
+    att_t,
+    got_sems,
+    in_sems,
+):
+    step = DEVICES // PIECES
+    got_copies = [
+        pltpu.make_async_copy(
+            got_ref.at[pl.ds(i * step, step)], got.at[pl.ds(i * step, step)], got_sems.at[i]
+        )
+        for i in range(PIECES)
+    ]
+    others = [
+        pltpu.make_async_copy(src, dst, in_sems.at[i])
+        for i, (src, dst) in enumerate(
+            [
+                (slots_ref, slots_buf),
+                (w_ref, w_buf),
+                (tokens_ref, tok_buf),
+                (gate_ref, gate_buf),
+            ]
+        )
+    ]
+    for copy in got_copies + others:
+        copy.start()
+    others[0].wait()
+    place = jnp.broadcast_to(place_of(slots_buf[...]), (BLK, BLK))
+    row_id = lax.broadcasted_iota(jnp.int32, (BLK, BLK), 0)
+    hot = jnp.where(place == row_id, 1.0, 0.0).T.astype(jnp.bfloat16)
     low = lax.broadcasted_iota(jnp.int32, (1, BLK), 1) < HALF
     for h in range(HEADS):
+        if h % (HEADS // PIECES) == 0:
+            got_copies[h // (HEADS // PIECES)].wait()
         halves = []
         for a in range(2):
-            parts = [got_ref[h * GROUPS + 2 * a + b].astype(jnp.float32) for b in range(2)]
+            parts = [got[h * GROUPS + 2 * a + b].astype(jnp.float32) for b in range(2)]
             lse = [p[32:33] + p[33:34] for p in parts]
             gap = jnp.broadcast_to(lse[1] - lse[0], (8, BLK))
             gap = jnp.where(low, roll(gap, HALF), gap)[:1]
@@ -284,42 +405,43 @@
         att_t[h * HD : (h + 1) * HD, :] = jnp.concatenate(
             [upper, lower[: HD - OUT_ROWS]], axis=0
         )
-    place = jnp.broadcast_to(place_of(slots_ref[...]), (BLK, BLK))
-    row_id = lax.broadcasted_iota(jnp.int32, (BLK, BLK), 0)
-    hot = jnp.where(place == row_id, 1.0, 0.0).T.astype(jnp.bfloat16)
     rows = lax.dot_general(
         hot,
         att_t[...].astype(jnp.bfloat16),
         (((1,), (1,)), ((), ())),
         preferred_element_type=jnp.float32,
     ).astype(jnp.bfloat16)
-    copy.wait()
+    for copy in others[1:]:
+        copy.wait()
     branch = jnp.dot(rows, w_buf[...], preferred_element_type=jnp.float32)
-    out_ref[...] = (tokens_ref[...].astype(jnp.float32) + gate_ref[...] * branch).astype(
-        jnp.bfloat16
-    )
+    out_ref[...] = (tok_buf[...].astype(jnp.float32) + gate_buf[...] * branch).astype(jnp.bfloat16)
 
 
 def vmem():
     return pl.BlockSpec(memory_space=pltpu.VMEM)
+
+
+def hbm():
+    return pl.BlockSpec(memory_space=pl.ANY)
 
 
 def pre(slots, tokens, shift, scale, w_qkv):
     return pl.pallas_call(
         pre_kernel,
         out_shape=jax.ShapeDtypeStruct((DEVICES, IN_ROWS, BLK), jnp.bfloat16),
-        in_specs=[
-            vmem(),
-            vmem(),
-            vmem(),
-            vmem(),
-            pl.BlockSpec(memory_space=pl.ANY),
-        ],
-        out_specs=vmem(),
+        in_specs=[hbm()] * 5,
+        out_specs=hbm(),
         scratch_shapes=[
-            pltpu.VMEM((W_CHUNKS, D, W_CHUNK), jnp.bfloat16),
-            pltpu.VMEM((3 * D, BLK), jnp.float32),
-            pltpu.SemaphoreType.DMA((W_CHUNKS,)),
+            pltpu.VMEM((BLK,), jnp.int32),
+            pltpu.VMEM((BLK, D), jnp.bfloat16),
+            pltpu.VMEM((D,), jnp.float32),
+            pltpu.VMEM((D,), jnp.float32),
+            pltpu.VMEM((3, D, D), jnp.bfloat16),
+            pltpu.VMEM((3, D, BLK), jnp.float32),
+            pltpu.VMEM((DEVICES, IN_ROWS, BLK), jnp.bfloat16),
+            pltpu.SemaphoreType.DMA((4,)),
+            pltpu.SemaphoreType.DMA((3,)),
+            pltpu.SemaphoreType.DMA((2,)),
         ],
         compiler_params=pltpu.CompilerParams(vmem_limit_bytes=VMEM),
         name="merge_norm_qkv",
@@ -330,11 +452,14 @@
     return pl.pallas_call(
         attend_kernel,
         out_shape=jax.ShapeDtypeStruct((DEVICES, OUT_ROWS, BLK), jnp.bfloat16),
-        in_specs=[vmem()],
-        out_specs=vmem(),
+        in_specs=[hbm()],
+        out_specs=hbm(),
         scratch_shapes=[
-            pltpu.VMEM((144, BLK), jnp.int32),
-            pltpu.SMEM((144, BLK), jnp.int32),
+            pltpu.VMEM((DEVICES, 16, BLK), jnp.bfloat16),
+            pltpu.VMEM((DEVICES, IN_ROWS, BLK), jnp.bfloat16),
+            pltpu.VMEM((DEVICES, OUT_ROWS, BLK), jnp.bfloat16),
+            pltpu.VMEM((16, BLK), jnp.int32),
+            pltpu.SMEM((16, BLK), jnp.int32),
             pltpu.VMEM((TILES, AUG, BLK), jnp.float32),
             pltpu.VMEM((TILES, HD, BLK), jnp.float32),
             pltpu.VMEM((TILES, HD, BLK), jnp.float32),
@@ -348,6 +473,9 @@
             pltpu.VMEM((Q_ROWS * Q_TILES, BLK), jnp.float32),
             pltpu.VMEM((TILES, AUG, BLK), jnp.float32),
             pltpu.SemaphoreType.DMA,
+            pltpu.SemaphoreType.DMA,
+            pltpu.SemaphoreType.DMA((PIECES,)),
+            pltpu.SemaphoreType.DMA((PIECES,)),
         ],
         compiler_params=pltpu.CompilerParams(vmem_limit_bytes=VMEM),
         name="attend_head",
@@ -358,12 +486,17 @@
     return pl.pallas_call(
         post_kernel,
         out_shape=jax.ShapeDtypeStruct((BLK, D), jnp.bfloat16),
-        in_specs=[vmem()] * 4 + [pl.BlockSpec(memory_space=pl.ANY)],
+        in_specs=[hbm()] * 5,
         out_specs=vmem(),
         scratch_shapes=[
+            pltpu.VMEM((DEVICES, OUT_ROWS, BLK), jnp.bfloat16),
+            pltpu.VMEM((BLK,), jnp.int32),
+            pltpu.VMEM((BLK, D), jnp.bfloat16),
+            pltpu.VMEM((D,), jnp.float32),
+            pltpu.VMEM((D, D), jnp.bfloat16),
             pltpu.VMEM((D, BLK), jnp.float32),
-            pltpu.VMEM((D, D), jnp.bfloat16),
-            pltpu.SemaphoreType.DMA,
+            pltpu.SemaphoreType.DMA((PIECES,)),
+            pltpu.SemaphoreType.DMA((4,)),
         ],
         compiler_params=pltpu.CompilerParams(vmem_limit_bytes=VMEM),
         name="combine_project",

time: 88.2 us -> 83.6 us (0.948)
  Pallas kernels: 28.8 us -> 24.1 us
    pallas_call x1, Pallas kernels: 16.8 us -> 14.1 us  [attend(): pl.pallas_call(attend_kernel, out_shape=jax.ShapeDtypeStruct((DEVICES, OU...]
    pallas_call x1, Pallas kernels: 7.73 us -> 6.18 us  [pre(): pl.pallas_call(pre_kernel, out_shape=jax.ShapeDtypeStruct((DEVICES, IN_RO...]
where the time goes in v3:
time: 83.6 us; the launch traced here: 83.3 us
  blocking collectives  59 us (71%)
  Pallas kernels  24.1 us (29%)
    all_to_all x1, blocking collectives, body(): got = lax.all_to_all(sent, 'patch', 0, 0, tiled=True)  38.8 us
    all_to_all x1, blocking collectives, body(): returned = lax.all_to_all(back, 'patch', 0, 0, tiled=True)  20.2 us
    pallas_call x1, Pallas kernels, attend(): pl.pallas_call(attend_kernel, out_shape=jax.ShapeDtypeStruct((DEVICES, OU...  14.1 us
    pallas_call x1, Pallas kernels, pre(): pl.pallas_call(pre_kernel, out_shape=jax.ShapeDtypeStruct((DEVICES, IN_RO...  6.18 us
    pallas_call x1, Pallas kernels, post(): pl.pallas_call(post_kernel, out_shape=jax.ShapeDtypeStruct((BLK, D), jnp....  3.82 us

profile of v3, /device:TPU:0, one launch (start us, length us, event | category | flops | bytes accessed | tf_op | source)
XLA Modules:
  0.0 83.3 jit_solution(15503524875881049334)
XLA Ops:
  0.0 6.2 %merge_norm_qkv.1 = bf16[64,112,128]{2,1,0:T(8,128)(2,1)} custom-call(s32[128]{0:T(128)} %slots_ref.3, bf16[128,1152]{1,0:T(8,128)(2,1)} %tokens_ref.3, f32[1152]{0:T(1024)} %shift_ref.1, f32[1152]{0:T(1024)} %scale_ref.1, bf16[1152,3456]{1,0:T(8,128)(2,1)} %w_ref.2), custom_call_target="tpu_custom_call" | custom-call | tf_op jit(solution)/shard_map/merge_norm_qkv/pallas_call | solution.py:429
  6.2 38.8 %all_to_all.10.got_ref = bf16[64,112,128]{2,1,0:T(8,128)(2,1)} all-to-all(bf16[64,112,128]{2,1,0:T(8,128)(2,1)} %merge_norm_qkv.1), channel_id=1, replica_groups=mesh['patch'=64,'batch'=2] {'patch'}, dimensions={0} | all-to-all | bytes 3670016 | tf_op jit(solution)/shard_map/all_to_all | solution.py:508
  45.0 14.1 %attend_head.1 = bf16[64,40,128]{2,1,0:T(8,128)(2,1)} custom-call(bf16[64,112,128]{2,1,0:T(8,128)(2,1)} %all_to_all.10.got_ref), custom_call_target="tpu_custom_call" | custom-call | tf_op jit(solution)/shard_map/attend_head/pallas_call | solution.py:452
  59.1 20.2 %all_to_all.11.got_ref = bf16[64,40,128]{2,1,0:T(8,128)(2,1)} all-to-all(bf16[64,40,128]{2,1,0:T(8,128)(2,1)} %attend_head.1), channel_id=1, replica_groups=mesh['patch'=64,'batch'=2] {'patch'}, dimensions={0} | all-to-all | bytes 1310720 | tf_op jit(solution)/shard_map/all_to_all | solution.py:510
  79.3 3.8 %combine_project.1 = bf16[128,1152]{1,0:T(8,128)(2,1)} custom-call(bf16[64,40,128]{2,1,0:T(8,128)(2,1)} %all_to_all.11.got_ref, s32[128]{0:T(128)} %slots_ref.3, bf16[128,1152]{1,0:T(8,128)(2,1)} %tokens_ref.3, f32[1152]{0:T(1024)} %gate_ref.1, bf16[1152,1152]{1,0:T(8,128)(2,1)} %w_ref.3), custom_call_target="tpu_custom_call" | custom-call | tf_op jit(solution)/shard_map/combine_project/pallas_call | solution.py:486

commit v4 on v3

--- a/solution.py
+++ b/solution.py
@@ -23,7 +23,7 @@
 PIECES = 4
 Q_TILES = 4
 EARLY = 64
-VMEM = 56 * 1024 * 1024
+MIB = 1024 * 1024
 
 INVERSE = 1.0 / HD**0.5
 LOG2E = 1.4426950408889634
@@ -161,9 +161,6 @@
 
 
 def attend_kernel(
-    got_ref,
-    out_ref,
-    tail,
     got,
     out,
     offs_v,
@@ -181,29 +178,13 @@
     done,
     done_t,
     sem,
-    tail_sem,
-    got_sems,
-    out_sems,
 ):
-    each = DEVICES // PIECES
-    pieces = [pl.ds(i * each, each) for i in range(PIECES)]
-    tail_copy = pltpu.make_async_copy(
-        got_ref.at[:, pl.ds(IN_ROWS - 16, 16)], tail, tail_sem
-    )
-    tail_copy.start()
-    got_copies = [
-        pltpu.make_async_copy(got_ref.at[p], got.at[p], got_sems.at[i])
-        for i, p in enumerate(pieces)
-    ]
-    for copy in got_copies:
-        copy.start()
     lane = lax.broadcasted_iota(jnp.int32, (1, BLK), 1)
     low = lane < HALF
 
     row = lax.broadcasted_iota(jnp.int32, (BLK, DEVICES * 16), 0)
     col = lax.broadcasted_iota(jnp.int32, (BLK, DEVICES * 16), 1)
-    tail_copy.wait()
-    last_rows = tail[...].reshape(DEVICES * 16, BLK)
+    last_rows = got[:, IN_ROWS - 16 :, :].reshape(DEVICES * 16, BLK)
     for x in range(2):
         before = (col < row * 16) & ((col & 15) == 9 + x)
         sums = jnp.dot(
@@ -240,9 +221,7 @@
         put(q_t, q_tile, 64, HD, roll(message[104:], q_off), keep_q)
         return 0
 
-    for i in range(PIECES):
-        got_copies[i].wait()
-        lax.fori_loop(i * each, (i + 1) * each, pack, 0, unroll=each)
+    lax.fori_loop(0, DEVICES, pack, 0, unroll=16)
 
     total = offs[0, DEVICES]
     line8 = lax.broadcasted_iota(jnp.int32, (8, BLK), 0)
@@ -338,59 +317,15 @@
         out[b] = jnp.where(low, first, second).astype(jnp.bfloat16)
         return 0
 
-    out_copies = []
-    for i, p in enumerate(pieces):
-        lax.fori_loop(i * each, (i + 1) * each, unpack, 0, unroll=each)
-        out_copies.append(pltpu.make_async_copy(out.at[p], out_ref.at[p], out_sems.at[i]))
-        out_copies[i].start()
-    for copy in out_copies:
-        copy.wait()
-
-
-def post_kernel(
-    got_ref,
-    slots_ref,
-    tokens_ref,
-    gate_ref,
-    w_ref,
-    out_ref,
-    got,
-    slots_buf,
-    tok_buf,
-    gate_buf,
-    w_buf,
-    att_t,
-    got_sems,
-    in_sems,
-):
-    step = DEVICES // PIECES
-    got_copies = [
-        pltpu.make_async_copy(
-            got_ref.at[pl.ds(i * step, step)], got.at[pl.ds(i * step, step)], got_sems.at[i]
-        )
-        for i in range(PIECES)
-    ]
-    others = [
-        pltpu.make_async_copy(src, dst, in_sems.at[i])
-        for i, (src, dst) in enumerate(
-            [
-                (slots_ref, slots_buf),
-                (w_ref, w_buf),
-                (tokens_ref, tok_buf),
-                (gate_ref, gate_buf),
-            ]
-        )
-    ]
-    for copy in got_copies + others:
-        copy.start()
-    others[0].wait()
-    place = jnp.broadcast_to(place_of(slots_buf[...]), (BLK, BLK))
+    lax.fori_loop(0, DEVICES, unpack, 0, unroll=16)
+
+
+def post_kernel(got, slots_ref, tokens_ref, gate_ref, w_ref, out_ref, att_t):
+    place = jnp.broadcast_to(place_of(slots_ref[...]), (BLK, BLK))
     row_id = lax.broadcasted_iota(jnp.int32, (BLK, BLK), 0)
     hot = jnp.where(place == row_id, 1.0, 0.0).T.astype(jnp.bfloat16)
     low = lax.broadcasted_iota(jnp.int32, (1, BLK), 1) < HALF
     for h in range(HEADS):
-        if h % (HEADS // PIECES) == 0:
-            got_copies[h // (HEADS // PIECES)].wait()
         halves = []
         for a in range(2):
             parts = [got[h * GROUPS + 2 * a + b].astype(jnp.float32) for b in range(2)]
@@ -411,10 +346,10 @@
         (((1,), (1,)), ((), ())),
         preferred_element_type=jnp.float32,
     ).astype(jnp.bfloat16)
-    for copy in others[1:]:
-        copy.wait()
-    branch = jnp.dot(rows, w_buf[...], preferred_element_type=jnp.float32)
-    out_ref[...] = (tok_buf[...].astype(jnp.float32) + gate_buf[...] * branch).astype(jnp.bfloat16)
+    branch = jnp.dot(rows, w_ref[...], preferred_element_type=jnp.float32)
+    out_ref[...] = (tokens_ref[...].astype(jnp.float32) + gate_ref[...] * branch).astype(
+        jnp.bfloat16
+    )
 
 
 def vmem():
@@ -443,7 +378,7 @@
             pltpu.SemaphoreType.DMA((3,)),
             pltpu.SemaphoreType.DMA((2,)),
         ],
-        compiler_params=pltpu.CompilerParams(vmem_limit_bytes=VMEM),
+        compiler_params=pltpu.CompilerParams(vmem_limit_bytes=56 * MIB),
         name="merge_norm_qkv",
     )(slots, tokens, shift, scale, w_qkv)
 
@@ -452,12 +387,9 @@
     return pl.pallas_call(
         attend_kernel,
         out_shape=jax.ShapeDtypeStruct((DEVICES, OUT_ROWS, BLK), jnp.bfloat16),
-        in_specs=[hbm()],
-        out_specs=hbm(),
+        in_specs=[vmem()],
+        out_specs=vmem(),
         scratch_shapes=[
-            pltpu.VMEM((DEVICES, 16, BLK), jnp.bfloat16),
-            pltpu.VMEM((DEVICES, IN_ROWS, BLK), jnp.bfloat16),
-            pltpu.VMEM((DEVICES, OUT_ROWS, BLK), jnp.bfloat16),
             pltpu.VMEM((16, BLK), jnp.int32),
             pltpu.SMEM((16, BLK), jnp.int32),
             pltpu.VMEM((TILES, AUG, BLK), jnp.float32),
@@ -473,11 +405,8 @@
             pltpu.VMEM((Q_ROWS * Q_TILES, BLK), jnp.float32),
             pltpu.VMEM((TILES, AUG, BLK), jnp.float32),
             pltpu.SemaphoreType.DMA,
-            pltpu.SemaphoreType.DMA,
-            pltpu.SemaphoreType.DMA((PIECES,)),
-            pltpu.SemaphoreType.DMA((PIECES,)),
         ],
-        compiler_params=pltpu.CompilerParams(vmem_limit_bytes=VMEM),
+        compiler_params=pltpu.CompilerParams(vmem_limit_bytes=30 * MIB),
         name="attend_head",
     )(got)
 
@@ -486,19 +415,10 @@
     return pl.pallas_call(
         post_kernel,
         out_shape=jax.ShapeDtypeStruct((BLK, D), jnp.bfloat16),
-        in_specs=[hbm()] * 5,
+        in_specs=[vmem()] * 5,
         out_specs=vmem(),
-        scratch_shapes=[
-            pltpu.VMEM((DEVICES, OUT_ROWS, BLK), jnp.bfloat16),
-            pltpu.VMEM((BLK,), jnp.int32),
-            pltpu.VMEM((BLK, D), jnp.bfloat16),
-            pltpu.VMEM((D,), jnp.float32),
-            pltpu.VMEM((D, D), jnp.bfloat16),
-            pltpu.VMEM((D, BLK), jnp.float32),
-            pltpu.SemaphoreType.DMA((PIECES,)),
-            pltpu.SemaphoreType.DMA((4,)),
-        ],
-        compiler_params=pltpu.CompilerParams(vmem_limit_bytes=VMEM),
+        scratch_shapes=[pltpu.VMEM((D, BLK), jnp.float32)],
+        compiler_params=pltpu.CompilerParams(vmem_limit_bytes=8 * MIB),
         name="combine_project",
     )(returned, slots, tokens, gate, w_out)
 

time: 83.6 us -> 78.9 us (0.944)
  Pallas kernels: 24.1 us -> 20 us
    pallas_call x1, Pallas kernels: 3.82 us -> 1.64 us  [post(): pl.pallas_call(post_kernel, out_shape=jax.ShapeDtypeStruct((BLK, D), jnp....]
    pallas_call x1, Pallas kernels: 14.1 us -> 12.2 us  [attend(): pl.pallas_call(attend_kernel, out_shape=jax.ShapeDtypeStruct((DEVICES, OU...]
where the time goes in v4:
time: 78.9 us; the launch traced here: 78.6 us
  blocking collectives  58.6 us (74%)
  Pallas kernels  20 us (25%)
    all_to_all x1, blocking collectives, body(): got = lax.all_to_all(sent, 'patch', 0, 0, tiled=True)  38.7 us
    all_to_all x1, blocking collectives, body(): returned = lax.all_to_all(back, 'patch', 0, 0, tiled=True)  19.9 us
    pallas_call x1, Pallas kernels, attend(): pl.pallas_call(attend_kernel, out_shape=jax.ShapeDtypeStruct((DEVICES, OU...  12.2 us
    pallas_call x1, Pallas kernels, pre(): pl.pallas_call(pre_kernel, out_shape=jax.ShapeDtypeStruct((DEVICES, IN_RO...  6.15 us
    pallas_call x1, Pallas kernels, post(): pl.pallas_call(post_kernel, out_shape=jax.ShapeDtypeStruct((BLK, D), jnp....  1.64 us

profile of v4, /device:TPU:0, one launch (start us, length us, event | category | flops | bytes accessed | tf_op | source)
XLA Modules:
  0.0 78.6 jit_solution(1408753718981233094)
XLA Ops:
  0.0 6.1 %merge_norm_qkv.1 = bf16[64,112,128]{2,1,0:T(8,128)(2,1)} custom-call(s32[128]{0:T(128)} %slots_ref.3, bf16[128,1152]{1,0:T(8,128)(2,1)} %tokens_ref.3, f32[1152]{0:T(1024)} %shift_ref.1, f32[1152]{0:T(1024)} %scale_ref.1, bf16[1152,3456]{1,0:T(8,128)(2,1)} %w_ref.2), custom_call_target="tpu_custom_call" | custom-call | tf_op jit(solution)/shard_map/merge_norm_qkv/pallas_call | solution.py:364
  6.2 38.7 %all_to_all.10.got = bf16[64,112,128]{2,1,0:T(8,128)(2,1)S(1)} all-to-all(bf16[64,112,128]{2,1,0:T(8,128)(2,1)} %merge_norm_qkv.1), channel_id=1, replica_groups=mesh['patch'=64,'batch'=2] {'patch'}, dimensions={0} | all-to-all | bytes 3670016 | tf_op jit(solution)/shard_map/all_to_all | solution.py:428
  44.9 0.0 copy-start
  44.9 0.0 copy-start.1
  44.9 0.0 copy-start.2
  44.9 0.0 copy-start.3
  44.9 12.2 %attend_head.1 = bf16[64,40,128]{2,1,0:T(8,128)(2,1)S(1)} custom-call(bf16[64,112,128]{2,1,0:T(8,128)(2,1)S(1)} %all_to_all.10.got), custom_call_target="tpu_custom_call" | custom-call | tf_op jit(solution)/shard_map/attend_head/pallas_call | solution.py:387
  57.1 19.9 %all_to_all.11.got = bf16[64,40,128]{2,1,0:T(8,128)(2,1)S(1)} all-to-all(bf16[64,40,128]{2,1,0:T(8,128)(2,1)S(1)} %attend_head.1), channel_id=1, replica_groups=mesh['patch'=64,'batch'=2] {'patch'}, dimensions={0} | all-to-all | bytes 1310720 | tf_op jit(solution)/shard_map/all_to_all | solution.py:430
  77.0 0.0 copy-done
  77.0 0.0 copy-done.1
  77.0 0.0 copy-done.2
  77.0 0.0 copy-done.3
  77.0 1.6 %combine_project.1 = bf16[128,1152]{1,0:T(8,128)(2,1)} custom-call(bf16[64,40,128]{2,1,0:T(8,128)(2,1)S(1)} %all_to_all.11.got, s32[128]{0:T(128)S(1)} %copy-done.3, bf16[128,1152]{1,0:T(8,128)(2,1)S(1)} %copy-done.1, f32[1152]{0:T(1024)S(1)} %copy-done.2, bf16[1152,1152]{1,0:T(8,128)(2,1)S(1)} %copy-done), custom_call_target="tpu_custom_call" | custom-call | tf_op jit(solution)/shard_map/combine_project/pallas_call | solution.py:415
Async XLA Ops:
  44.9 32.1 %copy-start = (bf16[1152,1152]{1,0:T(8,128)(2,1)S(1)}, bf16[1152,1152]{1,0:T(8,128)(2,1)}, u32[]{:S(2)}) copy-start(bf16[1152,1152]{1,0:T(8,128)(2,1)} %w_ref.3) | copy-start | bytes 7962628
  44.9 32.1 %copy-start.1 = (bf16[128,1152]{1,0:T(8,128)(2,1)S(1)}, bf16[128,1152]{1,0:T(8,128)(2,1)}, u32[]{:S(2)}) copy-start(bf16[128,1152]{1,0:T(8,128)(2,1)} %tokens_ref.3) | copy-start | bytes 884740
  44.9 32.1 %copy-start.2 = (f32[1152]{0:T(1024)S(1)}, f32[1152]{0:T(1024)}, u32[]{:S(2)}) copy-start(f32[1152]{0:T(1024)} %gate_ref.1) | copy-start | bytes 13828
  44.9 32.1 %copy-start.3 = (s32[128]{0:T(128)S(1)}, s32[128]{0:T(128)}, u32[]{:S(2)}) copy-start(s32[128]{0:T(128)} %slots_ref.3) | copy-start | bytes 1540

commit v5 on v4

--- a/solution.py
+++ b/solution.py
@@ -1,3 +1,5 @@
+import functools
+
 import jax
 import jax.numpy as jnp
 from jax import lax
@@ -19,9 +21,8 @@
 TILES = 22
 CHUNK = 2 * BLK
 COLUMNS = (TILES - 1) * BLK
-Q_ROWS = 656
-PIECES = 4
-Q_TILES = 4
+Q_TILES = (512, 640, 768, 672)
+UNROLL = 17
 EARLY = 64
 MIB = 1024 * 1024
 
@@ -118,9 +119,11 @@
             qkv_t[part, t * BLK : (t + 1) * BLK, :] = out[:, t * BLK : (t + 1) * BLK].T
 
     large[0].wait()
+    large[1].wait()
     project(1)
-    large[1].wait()
     project(2)
+    large[2].wait()
+    project(0)
     early = []
     for h in range(HEADS):
         k = qkv_t[1, h * HD : (h + 1) * HD, :]
@@ -134,8 +137,6 @@
         messages.at[:, pl.ds(0, EARLY)], out_ref.at[:, pl.ds(0, EARLY)], out_sems.at[0]
     )
     first.start()
-    large[2].wait()
-    project(0)
     for h in range(HEADS):
         q = qkv_t[0, h * HD : (h + 1) * HD, :]
         q_roll = roll(q, HALF)
@@ -214,36 +215,53 @@
         keep_k, keep_q = lane >= k_off, lane >= q_off
         k_over, q_over = (k_off + HALF) & 127, (q_off + HALF) & 127
         put(k_t, k_tile, 0, HD, roll(message[:HD], k_off), keep_k)
-        put(v_t, k_tile, 0, HD, roll(message[:HD], k_over), keep_k)
         put(k_t, k_tile, HD, AUG, roll(message[104:], k_over), keep_k)
         put(q_t, q_tile, 0, 32, roll(message[HD:104], q_off), keep_q)
         put(q_t, q_tile, 32, 64, roll(message[HD:104], q_over), keep_q)
         put(q_t, q_tile, 64, HD, roll(message[104:], q_off), keep_q)
         return 0
 
-    lax.fori_loop(0, DEVICES, pack, 0, unroll=16)
+    def pack_values(b):
+        at = offs[0, b]
+        tile, off = at >> 7, at & 127
+        moved = roll(got[b, :HD, :].astype(jnp.float32), (off + HALF) & 127)
+        put(v_t, tile, 0, HD, moved, lane >= off)
+
+    lax.fori_loop(0, DEVICES, pack, 0, unroll=32)
 
     total = offs[0, DEVICES]
     line8 = lax.broadcasted_iota(jnp.int32, (8, BLK), 0)
     zeros = jnp.zeros((BLK - AUG, BLK), jnp.float32)
     ones2 = jnp.where(line8 < 2, 1.0, 0.0)
     ones1 = jnp.where(line8 < 1, 1.0, 0.0)
-    for t in range(TILES - 1):
+    def set_keys(t):
         members = jnp.broadcast_to(k_t[t, HD : HD + 1, :], (8, BLK))
         bias = jnp.log(jnp.maximum(members, 1.0)) * (1.0 / INVERSE)
         bias = jnp.where(lane + t * BLK < total, bias, -1e30)
         high = bias.astype(jnp.bfloat16).astype(jnp.float32)
         rest = jnp.where(line8 == 0, high, jnp.where(line8 == 1, bias - high, 0.0))
-        k_tile, v_tile, q_tile = k_t[t, :HD, :], v_t[t, :HD, :], q_t[t, :HD, :]
-        cols = slice(t * BLK, (t + 1) * BLK)
-        keys[:, cols] = jnp.concatenate([k_tile, rest, zeros], axis=0).astype(jnp.bfloat16)
-        vals[cols, :] = jnp.concatenate([v_tile, ones1, zeros], axis=0).T.astype(jnp.bfloat16)
-        queries[cols, :] = jnp.concatenate([q_tile, ones2, zeros], axis=0).T.astype(jnp.bfloat16)
+        keys[:, t * BLK : (t + 1) * BLK] = jnp.concatenate(
+            [k_t[t, :HD, :], rest, zeros], axis=0
+        ).astype(jnp.bfloat16)
+
+    def set_queries(t):
+        queries[t * BLK : (t + 1) * BLK, :] = jnp.concatenate(
+            [q_t[t, :HD, :], ones2, zeros], axis=0
+        ).T.astype(jnp.bfloat16)
+
+    def set_values(t):
+        vals[t * BLK : (t + 1) * BLK, :] = jnp.concatenate(
+            [v_t[t, :HD, :], ones1, zeros], axis=0
+        ).T.astype(jnp.bfloat16)
+
+    for t in range(TILES - 1):
+        set_keys(t)
+    early = Q_TILES[0] // BLK
+    for t in range(early):
+        set_queries(t)
 
     chunks = [slice(at, min(at + CHUNK, COLUMNS)) for at in range(0, COLUMNS, CHUNK)]
-
-    def rows_of(i):
-        return pl.ds(pl.multiple_of(i * Q_ROWS, 16), Q_ROWS)
+    starts = [sum(Q_TILES[:i]) for i in range(len(Q_TILES) + 1)]
 
     def fold(s, best):
         for t in range(s.shape[1] // BLK):
@@ -251,62 +269,14 @@
             best = part if best is None else jnp.maximum(best, part)
         return best
 
-    def step(i, scores, top, ahead_scores, ahead_top):
-        best = None
-        o = None
-        q = queries[rows_of(i + 1), :] if ahead_scores is not None else None
-        for c in chunks:
-            if ahead_scores is not None:
-                s = jnp.dot(q, keys[:, c], preferred_element_type=jnp.float32)
-                ahead_scores[:, c] = s
-                best = fold(s, best)
-            if scores is not None:
-                n = (c.stop - c.start) // BLK
-                p = [
-                    jnp.exp2(
-                        (scores[:, c.start + t * BLK : c.start + (t + 1) * BLK] - top[...])
-                        * (INVERSE * LOG2E)
-                    ).astype(jnp.bfloat16)
-                    for t in range(n)
-                ]
-                p = jnp.concatenate(p, axis=1)
-                part = jnp.dot(p, vals[c, :], preferred_element_type=jnp.float32)
-                o = part if o is None else o + part
-        if ahead_scores is not None:
-            ahead_top[...] = jnp.broadcast_to(
-                jnp.max(best, axis=1, keepdims=True), (Q_ROWS, BLK)
-            )
-        if scores is not None:
-            mass = jnp.broadcast_to(o[:, HD : HD + 1], (Q_ROWS, BLK))
-            lse = top[...] * INVERSE + jnp.log(mass)
-            high = lse.astype(jnp.bfloat16).astype(jnp.float32)
-            done[rows_of(i), :] = jnp.where(
-                lane < HD, o / mass, jnp.where(lane == HD, high, lse - high)
-            )
-
-    def two(i, _):
-        step(2 * i, scores_a, top_a, scores_b, top_b)
-        step(2 * i + 1, scores_b, top_b, scores_a, top_a)
-        return 0
-
-    step(-1, None, None, scores_a, top_a)
-    pairs = (Q_TILES - 1) // 2
-    lax.fori_loop(0, pairs, two, 0)
-    if Q_TILES % 2 == 0:
-        step(Q_TILES - 2, scores_a, top_a, scores_b, top_b)
-        step(Q_TILES - 1, scores_b, top_b, None, None)
-    else:
-        step(Q_TILES - 1, scores_a, top_a, None, None)
-
-    for t in range(TILES - 1):
-        last = min((t + 1) * BLK, Q_TILES * Q_ROWS)
+    def turn(t):
+        last = min((t + 1) * BLK, starts[-1])
         tile = done[t * BLK : last, :]
         if last < (t + 1) * BLK:
             tile = jnp.concatenate(
                 [tile, jnp.zeros(((t + 1) * BLK - last, BLK), jnp.float32)], axis=0
             )
         done_t[t] = tile.T[:AUG]
-    done_t[TILES - 1] = jnp.zeros((AUG, BLK), jnp.float32)
 
     def unpack(b, _):
         at = offs[8, b]
@@ -317,7 +287,62 @@
         out[b] = jnp.where(low, first, second).astype(jnp.bfloat16)
         return 0
 
-    lax.fori_loop(0, DEVICES, unpack, 0, unroll=16)
+    def step(i, beside):
+        scores, top = (scores_a, top_a) if i % 2 == 0 else (scores_b, top_b)
+        ahead_scores, ahead_top = (scores_b, top_b) if i % 2 == 0 else (scores_a, top_a)
+        n = Q_TILES[i] if i >= 0 else 0
+        m = Q_TILES[i + 1] if i + 1 < len(Q_TILES) else 0
+        best = None
+        o = None
+        q = queries[starts[i + 1] : starts[i + 1] + m, :] if m else None
+        each = -(-len(beside) // len(chunks))
+        for x, c in enumerate(chunks):
+            for work in beside[x * each : (x + 1) * each]:
+                work()
+            if m:
+                s = jnp.dot(q, keys[:, c], preferred_element_type=jnp.float32)
+                ahead_scores[:m, c] = s
+                best = fold(s, best)
+            if n:
+                p = [
+                    jnp.exp2(
+                        (scores[:n, at : at + BLK] - top[:n]) * (INVERSE * LOG2E)
+                    ).astype(jnp.bfloat16)
+                    for at in range(c.start, c.stop, BLK)
+                ]
+                p = jnp.concatenate(p, axis=1)
+                part = jnp.dot(p, vals[c, :], preferred_element_type=jnp.float32)
+                o = part if o is None else o + part
+        if m:
+            ahead_top[:m] = jnp.broadcast_to(jnp.max(best, axis=1, keepdims=True), (m, BLK))
+        if n:
+            mass = jnp.broadcast_to(o[:, HD : HD + 1], (n, BLK))
+            lse = top[:n] * INVERSE + jnp.log(mass)
+            high = lse.astype(jnp.bfloat16).astype(jnp.float32)
+            done[starts[i] : starts[i + 1], :] = jnp.where(
+                lane < HD, o / mass, jnp.where(lane == HD, high, lse - high)
+            )
+
+    turned = 0
+    unpacked = 0
+    done_t[TILES - 1] = jnp.zeros((AUG, BLK), jnp.float32)
+    for i in range(-1, len(Q_TILES)):
+        beside = []
+        if i < 0:
+            beside += [functools.partial(pack_values, b) for b in range(DEVICES)]
+            beside += [functools.partial(set_queries, t) for t in range(early, TILES - 1)]
+            beside += [functools.partial(set_values, t) for t in range(TILES - 1)]
+        if i >= 1:
+            for t in range(turned, starts[i] // BLK):
+                beside.append(functools.partial(turn, t))
+            turned = starts[i] // BLK
+            for b in range(unpacked, turned * BLK // HALF):
+                beside.append(functools.partial(unpack, b, 0))
+            unpacked = turned * BLK // HALF
+        step(i, beside)
+    for t in range(turned, TILES - 1):
+        turn(t)
+    lax.fori_loop(unpacked, DEVICES, unpack, 0, unroll=UNROLL)
 
 
 def post_kernel(got, slots_ref, tokens_ref, gate_ref, w_ref, out_ref, att_t):
@@ -398,11 +423,11 @@
             pltpu.VMEM((BLK, COLUMNS), jnp.bfloat16),
             pltpu.VMEM((COLUMNS, BLK), jnp.bfloat16),
             pltpu.VMEM((COLUMNS, BLK), jnp.bfloat16),
-            pltpu.VMEM((Q_ROWS, COLUMNS), jnp.float32),
-            pltpu.VMEM((Q_ROWS, COLUMNS), jnp.float32),
-            pltpu.VMEM((Q_ROWS, BLK), jnp.float32),
-            pltpu.VMEM((Q_ROWS, BLK), jnp.float32),
-            pltpu.VMEM((Q_ROWS * Q_TILES, BLK), jnp.float32),
+            pltpu.VMEM((max(Q_TILES), COLUMNS), jnp.float32),
+            pltpu.VMEM((max(Q_TILES), COLUMNS), jnp.float32),
+            pltpu.VMEM((max(Q_TILES), BLK), jnp.float32),
+            pltpu.VMEM((max(Q_TILES), BLK), jnp.float32),
+            pltpu.VMEM((sum(Q_TILES), BLK), jnp.float32),
             pltpu.VMEM((TILES, AUG, BLK), jnp.float32),
             pltpu.SemaphoreType.DMA,
         ],

time: 78.9 us -> 77.9 us (0.987)
  Pallas kernels: 20 us -> 19.1 us
where the time goes in v5:
time: 77.9 us; the launch traced here: 77.7 us
  blocking collectives  58.5 us (75%)
  Pallas kernels  19.1 us (25%)
    all_to_all x1, blocking collectives, body(): got = lax.all_to_all(sent, 'patch', 0, 0, tiled=True)  38.7 us
    all_to_all x1, blocking collectives, body(): returned = lax.all_to_all(back, 'patch', 0, 0, tiled=True)  19.8 us
    pallas_call x1, Pallas kernels, attend(): pl.pallas_call(attend_kernel, out_shape=jax.ShapeDtypeStruct((DEVICES, OU...  11.7 us
    pallas_call x1, Pallas kernels, pre(): pl.pallas_call(pre_kernel, out_shape=jax.ShapeDtypeStruct((DEVICES, IN_RO...  5.78 us
    pallas_call x1, Pallas kernels, post(): pl.pallas_call(post_kernel, out_shape=jax.ShapeDtypeStruct((BLK, D), jnp....  1.64 us

profile of v5, /device:TPU:0, one launch (start us, length us, event | category | flops | bytes accessed | tf_op | source)
XLA Modules:
  0.0 77.7 jit_solution(16848436499270199103)
XLA Ops:
  0.0 5.8 %merge_norm_qkv.1 = bf16[64,112,128]{2,1,0:T(8,128)(2,1)} custom-call(s32[128]{0:T(128)} %slots_ref.3, bf16[128,1152]{1,0:T(8,128)(2,1)} %tokens_ref.3, f32[1152]{0:T(1024)} %shift_ref.1, f32[1152]{0:T(1024)} %scale_ref.1, bf16[1152,3456]{1,0:T(8,128)(2,1)} %w_ref.2), custom_call_target="tpu_custom_call" | custom-call | tf_op jit(solution)/shard_map/merge_norm_qkv/pallas_call | solution.py:389
  5.8 38.7 %all_to_all.10.got = bf16[64,112,128]{2,1,0:T(8,128)(2,1)S(1)} all-to-all(bf16[64,112,128]{2,1,0:T(8,128)(2,1)} %merge_norm_qkv.1), channel_id=1, replica_groups=mesh['patch'=64,'batch'=2] {'patch'}, dimensions={0} | all-to-all | bytes 3670016 | tf_op jit(solution)/shard_map/all_to_all | solution.py:453
  44.5 0.0 copy-start
  44.5 0.0 copy-start.1
  44.5 0.0 copy-start.2
  44.5 0.0 copy-start.3
  44.5 11.7 %attend_head.1 = bf16[64,40,128]{2,1,0:T(8,128)(2,1)S(1)} custom-call(bf16[64,112,128]{2,1,0:T(8,128)(2,1)S(1)} %all_to_all.10.got), custom_call_target="tpu_custom_call" | custom-call | tf_op jit(solution)/shard_map/attend_head/pallas_call | solution.py:412
  56.2 19.8 %all_to_all.11.got = bf16[64,40,128]{2,1,0:T(8,128)(2,1)S(1)} all-to-all(bf16[64,40,128]{2,1,0:T(8,128)(2,1)S(1)} %attend_head.1), channel_id=1, replica_groups=mesh['patch'=64,'batch'=2] {'patch'}, dimensions={0} | all-to-all | bytes 1310720 | tf_op jit(solution)/shard_map/all_to_all | solution.py:455
  76.0 0.0 copy-done
  76.0 0.0 copy-done.1
  76.1 0.0 copy-done.2
  76.1 0.0 copy-done.3
  76.1 1.6 %combine_project.1 = bf16[128,1152]{1,0:T(8,128)(2,1)} custom-call(bf16[64,40,128]{2,1,0:T(8,128)(2,1)S(1)} %all_to_all.11.got, s32[128]{0:T(128)S(1)} %copy-done.3, bf16[128,1152]{1,0:T(8,128)(2,1)S(1)} %copy-done.1, f32[1152]{0:T(1024)S(1)} %copy-done.2, bf16[1152,1152]{1,0:T(8,128)(2,1)S(1)} %copy-done), custom_call_target="tpu_custom_call" | custom-call | tf_op jit(solution)/shard_map/combine_project/pallas_call | solution.py:440
Async XLA Ops:
  44.5 31.6 %copy-start = (bf16[1152,1152]{1,0:T(8,128)(2,1)S(1)}, bf16[1152,1152]{1,0:T(8,128)(2,1)}, u32[]{:S(2)}) copy-start(bf16[1152,1152]{1,0:T(8,128)(2,1)} %w_ref.3) | copy-start | bytes 7962628
  44.5 31.6 %copy-start.1 = (bf16[128,1152]{1,0:T(8,128)(2,1)S(1)}, bf16[128,1152]{1,0:T(8,128)(2,1)}, u32[]{:S(2)}) copy-start(bf16[128,1152]{1,0:T(8,128)(2,1)} %tokens_ref.3) | copy-start | bytes 884740
  44.5 31.6 %copy-start.2 = (f32[1152]{0:T(1024)S(1)}, f32[1152]{0:T(1024)}, u32[]{:S(2)}) copy-start(f32[1152]{0:T(1024)} %gate_ref.1) | copy-start | bytes 13828
  44.5 31.6 %copy-start.3 = (s32[128]{0:T(128)S(1)}, s32[128]{0:T(128)}, u32[]{:S(2)}) copy-start(s32[128]{0:T(128)} %slots_ref.3) | copy-start | bytes 1540

commit v6 on v5

--- a/solution.py
+++ b/solution.py
@@ -19,7 +19,7 @@
 OUT_ROWS = 40
 AUG = 80
 TILES = 22
-CHUNK = 2 * BLK
+CHUNK = 4 * BLK
 COLUMNS = (TILES - 1) * BLK
 Q_TILES = (512, 640, 768, 672)
 UNROLL = 17
@@ -73,8 +73,8 @@
         pltpu.make_async_copy(w_ref.at[:, pl.ds(part * D, D)], w_buf.at[part], w_sems.at[part])
         for part in (1, 2, 0)
     ]
-    for copy in large:
-        copy.start()
+    large[0].start()
+    large[1].start()
 
     small[0].wait()
     place = jnp.broadcast_to(place_of(slots_buf[...]), (BLK, BLK))
@@ -104,6 +104,7 @@
 
     for copy in small[1:]:
         copy.wait()
+    large[2].start()
     sums = jnp.dot(hot.astype(jnp.bfloat16), tok_buf[...], preferred_element_type=jnp.float32)
     values = (sums / jnp.maximum(members, 1.0)).astype(jnp.bfloat16).astype(jnp.float32)
     center = jnp.mean(values, axis=-1, keepdims=True)

time: 77.9 us -> 77.5 us (level)
  no operation moved by 1% of the time
where the time goes in v6:
time: 77.5 us; the launch traced here: 77.2 us
  blocking collectives  58.6 us (76%)
  Pallas kernels  18.6 us (24%)
    all_to_all x1, blocking collectives, body(): got = lax.all_to_all(sent, 'patch', 0, 0, tiled=True)  38.7 us
    all_to_all x1, blocking collectives, body(): returned = lax.all_to_all(back, 'patch', 0, 0, tiled=True)  19.9 us
    pallas_call x1, Pallas kernels, attend(): pl.pallas_call(attend_kernel, out_shape=jax.ShapeDtypeStruct((DEVICES, OU...  11.4 us
    pallas_call x1, Pallas kernels, pre(): pl.pallas_call(pre_kernel, out_shape=jax.ShapeDtypeStruct((DEVICES, IN_RO...  5.59 us
    pallas_call x1, Pallas kernels, post(): pl.pallas_call(post_kernel, out_shape=jax.ShapeDtypeStruct((BLK, D), jnp....  1.64 us

profile of v6, /device:TPU:0, one launch (start us, length us, event | category | flops | bytes accessed | tf_op | source)
XLA Modules:
  0.0 77.2 jit_solution(16671537376805651983)
XLA Ops:
  0.0 5.6 %merge_norm_qkv.1 = bf16[64,112,128]{2,1,0:T(8,128)(2,1)} custom-call(s32[128]{0:T(128)} %slots_ref.3, bf16[128,1152]{1,0:T(8,128)(2,1)} %tokens_ref.3, f32[1152]{0:T(1024)} %shift_ref.1, f32[1152]{0:T(1024)} %scale_ref.1, bf16[1152,3456]{1,0:T(8,128)(2,1)} %w_ref.2), custom_call_target="tpu_custom_call" | custom-call | tf_op jit(solution)/shard_map/merge_norm_qkv/pallas_call | solution.py:390
  5.6 38.7 %all_to_all.10.got = bf16[64,112,128]{2,1,0:T(8,128)(2,1)S(1)} all-to-all(bf16[64,112,128]{2,1,0:T(8,128)(2,1)} %merge_norm_qkv.1), channel_id=1, replica_groups=mesh['patch'=64,'batch'=2] {'patch'}, dimensions={0} | all-to-all | bytes 3670016 | tf_op jit(solution)/shard_map/all_to_all | solution.py:454
  44.3 0.0 copy-start
  44.3 0.0 copy-start.1
  44.3 0.0 copy-start.2
  44.3 0.0 copy-start.3
  44.3 11.4 %attend_head.1 = bf16[64,40,128]{2,1,0:T(8,128)(2,1)S(1)} custom-call(bf16[64,112,128]{2,1,0:T(8,128)(2,1)S(1)} %all_to_all.10.got), custom_call_target="tpu_custom_call" | custom-call | tf_op jit(solution)/shard_map/attend_head/pallas_call | solution.py:413
  55.7 19.9 %all_to_all.11.got = bf16[64,40,128]{2,1,0:T(8,128)(2,1)S(1)} all-to-all(bf16[64,40,128]{2,1,0:T(8,128)(2,1)S(1)} %attend_head.1), channel_id=1, replica_groups=mesh['patch'=64,'batch'=2] {'patch'}, dimensions={0} | all-to-all | bytes 1310720 | tf_op jit(solution)/shard_map/all_to_all | solution.py:456
  75.6 0.0 copy-done
  75.6 0.0 copy-done.1
  75.6 0.0 copy-done.2
  75.6 0.0 copy-done.3
  75.6 1.6 %combine_project.1 = bf16[128,1152]{1,0:T(8,128)(2,1)} custom-call(bf16[64,40,128]{2,1,0:T(8,128)(2,1)S(1)} %all_to_all.11.got, s32[128]{0:T(128)S(1)} %copy-done.3, bf16[128,1152]{1,0:T(8,128)(2,1)S(1)} %copy-done.1, f32[1152]{0:T(1024)S(1)} %copy-done.2, bf16[1152,1152]{1,0:T(8,128)(2,1)S(1)} %copy-done), custom_call_target="tpu_custom_call" | custom-call | tf_op jit(solution)/shard_map/combine_project/pallas_call | solution.py:441
Async XLA Ops:
  44.3 31.3 %copy-start = (bf16[1152,1152]{1,0:T(8,128)(2,1)S(1)}, bf16[1152,1152]{1,0:T(8,128)(2,1)}, u32[]{:S(2)}) copy-start(bf16[1152,1152]{1,0:T(8,128)(2,1)} %w_ref.3) | copy-start | bytes 7962628
  44.3 31.3 %copy-start.1 = (bf16[128,1152]{1,0:T(8,128)(2,1)S(1)}, bf16[128,1152]{1,0:T(8,128)(2,1)}, u32[]{:S(2)}) copy-start(bf16[128,1152]{1,0:T(8,128)(2,1)} %tokens_ref.3) | copy-start | bytes 884740
  44.3 31.3 %copy-start.2 = (f32[1152]{0:T(1024)S(1)}, f32[1152]{0:T(1024)}, u32[]{:S(2)}) copy-start(f32[1152]{0:T(1024)} %gate_ref.1) | copy-start | bytes 13828
  44.3 31.3 %copy-start.3 = (s32[128]{0:T(128)S(1)}, s32[128]{0:T(128)}, u32[]{:S(2)}) copy-start(s32[128]{0:T(128)} %slots_ref.3) | copy-start | bytes 1540

commit v7 on v6

--- a/solution.py
+++ b/solution.py
@@ -21,8 +21,8 @@
 TILES = 22
 CHUNK = 4 * BLK
 COLUMNS = (TILES - 1) * BLK
-Q_TILES = (512, 640, 768, 672)
-UNROLL = 17
+Q_TILES = (512, 896, 768, 416)
+UNROLL = 30
 EARLY = 64
 MIB = 1024 * 1024
 
@@ -432,7 +432,7 @@
             pltpu.VMEM((TILES, AUG, BLK), jnp.float32),
             pltpu.SemaphoreType.DMA,
         ],
-        compiler_params=pltpu.CompilerParams(vmem_limit_bytes=30 * MIB),
+        compiler_params=pltpu.CompilerParams(vmem_limit_bytes=34 * MIB),
         name="attend_head",
     )(got)
 

time: 77.5 us -> 77.3 us (level)
  no operation moved by 1% of the time
where the time goes in v7:
time: 77.3 us; the launch traced here: 77.1 us
  blocking collectives  58.6 us (76%)
  Pallas kernels  18.5 us (24%)
    all_to_all x1, blocking collectives, body(): got = lax.all_to_all(sent, 'patch', 0, 0, tiled=True)  38.7 us
    all_to_all x1, blocking collectives, body(): returned = lax.all_to_all(back, 'patch', 0, 0, tiled=True)  19.9 us
    pallas_call x1, Pallas kernels, attend(): pl.pallas_call(attend_kernel, out_shape=jax.ShapeDtypeStruct((DEVICES, OU...  11.2 us
    pallas_call x1, Pallas kernels, pre(): pl.pallas_call(pre_kernel, out_shape=jax.ShapeDtypeStruct((DEVICES, IN_RO...  5.59 us
    pallas_call x1, Pallas kernels, post(): pl.pallas_call(post_kernel, out_shape=jax.ShapeDtypeStruct((BLK, D), jnp....  1.64 us

profile of v7, /device:TPU:0, one launch (start us, length us, event | category | flops | bytes accessed | tf_op | source)
XLA Modules:
  0.0 77.1 jit_solution(533978684146697817)
XLA Ops:
  0.0 5.6 %merge_norm_qkv.1 = bf16[64,112,128]{2,1,0:T(8,128)(2,1)} custom-call(s32[128]{0:T(128)} %slots_ref.3, bf16[128,1152]{1,0:T(8,128)(2,1)} %tokens_ref.3, f32[1152]{0:T(1024)} %shift_ref.1, f32[1152]{0:T(1024)} %scale_ref.1, bf16[1152,3456]{1,0:T(8,128)(2,1)} %w_ref.2), custom_call_target="tpu_custom_call" | custom-call | tf_op jit(solution)/shard_map/merge_norm_qkv/pallas_call | solution.py:390
  5.6 38.7 %all_to_all.10.got = bf16[64,112,128]{2,1,0:T(8,128)(2,1)S(1)} all-to-all(bf16[64,112,128]{2,1,0:T(8,128)(2,1)} %merge_norm_qkv.1), channel_id=1, replica_groups=mesh['patch'=64,'batch'=2] {'patch'}, dimensions={0} | all-to-all | bytes 3670016 | tf_op jit(solution)/shard_map/all_to_all | solution.py:454
  44.3 0.0 copy-start
  44.3 0.0 copy-start.1
  44.3 0.0 copy-start.2
  44.3 0.0 copy-start.3
  44.3 11.2 %attend_head.1 = bf16[64,40,128]{2,1,0:T(8,128)(2,1)S(1)} custom-call(bf16[64,112,128]{2,1,0:T(8,128)(2,1)S(1)} %all_to_all.10.got), custom_call_target="tpu_custom_call" | custom-call | tf_op jit(solution)/shard_map/attend_head/pallas_call | solution.py:413
  55.6 19.9 %all_to_all.11.got = bf16[64,40,128]{2,1,0:T(8,128)(2,1)S(1)} all-to-all(bf16[64,40,128]{2,1,0:T(8,128)(2,1)S(1)} %attend_head.1), channel_id=1, replica_groups=mesh['patch'=64,'batch'=2] {'patch'}, dimensions={0} | all-to-all | bytes 1310720 | tf_op jit(solution)/shard_map/all_to_all | solution.py:456
  75.4 0.0 copy-done
  75.4 0.0 copy-done.1
  75.4 0.0 copy-done.2
  75.4 0.0 copy-done.3
  75.5 1.6 %combine_project.1 = bf16[128,1152]{1,0:T(8,128)(2,1)} custom-call(bf16[64,40,128]{2,1,0:T(8,128)(2,1)S(1)} %all_to_all.11.got, s32[128]{0:T(128)S(1)} %copy-done.3, bf16[128,1152]{1,0:T(8,128)(2,1)S(1)} %copy-done.1, f32[1152]{0:T(1024)S(1)} %copy-done.2, bf16[1152,1152]{1,0:T(8,128)(2,1)S(1)} %copy-done), custom_call_target="tpu_custom_call" | custom-call | tf_op jit(solution)/shard_map/combine_project/pallas_call | solution.py:441
Async XLA Ops:
  44.3 31.1 %copy-start = (bf16[1152,1152]{1,0:T(8,128)(2,1)S(1)}, bf16[1152,1152]{1,0:T(8,128)(2,1)}, u32[]{:S(2)}) copy-start(bf16[1152,1152]{1,0:T(8,128)(2,1)} %w_ref.3) | copy-start | bytes 7962628
  44.3 31.1 %copy-start.1 = (bf16[128,1152]{1,0:T(8,128)(2,1)S(1)}, bf16[128,1152]{1,0:T(8,128)(2,1)}, u32[]{:S(2)}) copy-start(bf16[128,1152]{1,0:T(8,128)(2,1)} %tokens_ref.3) | copy-start | bytes 884740
  44.3 31.1 %copy-start.2 = (f32[1152]{0:T(1024)S(1)}, f32[1152]{0:T(1024)}, u32[]{:S(2)}) copy-start(f32[1152]{0:T(1024)} %gate_ref.1) | copy-start | bytes 13828
  44.3 31.1 %copy-start.3 = (s32[128]{0:T(128)S(1)}, s32[128]{0:T(128)}, u32[]{:S(2)}) copy-start(s32[128]{0:T(128)} %slots_ref.3) | copy-start | bytes 1540
